TPU v7x, 128 devices: a whole 4x4x4 slice. The times are simulated.
128 devices in a mesh: ia: 8 (over z, x_hi), ja: 16 (over y, x_lo, core).
Axes of the slice: x: 4 (x_hi: 2, x_lo: 2; x = x_hi * 2 + x_lo), y: 4, z: 4, core: 2. Of those that a mesh axis runs over, the one named last changes fastest.
Arguments:
- positions: float32 [3, 196608], P(None, ('ia', 'ja')), may hold values from -6 to 6
- velocities: float32 [3, 196608], P(None, ('ia', 'ja')), may hold values from -6 to 6
- old_acc: float32 [3, 196608], P(None, ('ia', 'ja')), may hold values from -4 to 4
- old_jerk: float32 [3, 196608], P(None, ('ia', 'ja')), may hold values from -4 to 4
- masses: float32 [196608], P(('ia', 'ja')), may hold values from 0.1 to 10
- elapsed: float32 [196608], P(('ia', 'ja')), may hold values from 0 to 0.5
- levels: int32 [196608], P(('ia', 'ja')), may hold values from 0 to 3
- active_index: int32 [128, 512], P(('ia', 'ja')), may hold values from 0 to 1535, as said below
- active_count: int32 [128], P(('ia', 'ja')), may hold values from 1 to 512, as said below
Outputs:
- new_state: float32 [12, 65536], P(None, ('ia', 'ja'))
Inputs may be any that keep to these rules, and one draw needn't show every extreme that they name: `active_index`: within a row all 512 entries differ, also in slots that are not live. `active_count`: one owner has exactly 512 active stars and another exactly 1.
All inputs are finite; a program needn't handle non-finite values.
Results may differ from a plain program's by a relative error of at most 0.00002.
Values sent between devices are 32-bit elements; how exact they have to be, the bound alone decides.
A program may use at most 128 MiB of HBM per device.

v0:
```python
import jax
import jax.numpy as jnp
from jax import lax
from jax.sharding import PartitionSpec as P

soften = 0.01
step_max = 0.5


def predict(positions, velocities, old_acc, old_jerk, interval):
    tau_sq = 0.5 * interval * interval
    tau_cube = interval * interval * interval / 6.0
    pred_pos = positions + interval * velocities + tau_sq * old_acc + tau_cube * old_jerk
    pred_vel = velocities + interval * old_acc + tau_sq * old_jerk
    return (pred_pos, pred_vel)


def pair_sums(sources, targets):
    gap_x = sources[0][:, None] - targets[0][None, :]
    gap_y = sources[1][:, None] - targets[1][None, :]
    gap_z = sources[2][:, None] - targets[2][None, :]
    drift_x = sources[3][:, None] - targets[3][None, :]
    drift_y = sources[4][:, None] - targets[4][None, :]
    drift_z = sources[5][:, None] - targets[5][None, :]
    dist_sq = gap_x * gap_x + gap_y * gap_y + gap_z * gap_z + soften
    inverse = lax.rsqrt(dist_sq)
    weighted = inverse * inverse * inverse * sources[6][:, None]
    radial = 3.0 * (gap_x * drift_x + gap_y * drift_y + gap_z * drift_z) / dist_sq
    return jnp.stack(
        [
            jnp.sum(gap_x * weighted, axis=0),
            jnp.sum(gap_y * weighted, axis=0),
            jnp.sum(gap_z * weighted, axis=0),
            jnp.sum((drift_x - radial * gap_x) * weighted, axis=0),
            jnp.sum((drift_y - radial * gap_y) * weighted, axis=0),
            jnp.sum((drift_z - radial * gap_z) * weighted, axis=0),
        ]
    )


def blocked_sums(sources, targets, block_size):
    columns = targets.shape[1]
    pieces = targets.reshape(6, columns // block_size, block_size).transpose(1, 0, 2)
    result = lax.map(lambda piece: pair_sums(sources, piece), pieces)
    return result.transpose(1, 0, 2).reshape(6, columns)


def correct(start_pos, start_vel, start_acc, start_jerk, new_acc, new_jerk, step):
    new_vel = (
        start_vel
        + (start_acc + new_acc) * step / 2.0
        + (start_jerk - new_jerk) * step * step / 12.0
    )
    new_pos = (
        start_pos + (start_vel + new_vel) * step / 2.0 + (start_acc - new_acc) * step * step / 12.0
    )
    return (new_pos, new_vel)


def shards(
    positions, velocities, old_acc, old_jerk, masses, elapsed, levels, active_index, active_count
):
    stars_dev = masses.shape[0]
    slot_count = active_index.shape[1]
    local_index = active_index[0]
    live = jnp.arange(slot_count, dtype=jnp.int32) < active_count[0]
    matches = (local_index[:, None] == jnp.arange(stars_dev, dtype=jnp.int32)[None, :]) & live[
        :, None
    ]
    chosen = jnp.any(matches, axis=0)
    level_step = step_max * jnp.exp2(-levels.astype(jnp.float32))
    interval = jnp.where(chosen, level_step, elapsed)
    pred_pos, pred_vel = predict(positions, velocities, old_acc, old_jerk, interval)
    sources = jnp.concatenate([pred_pos, pred_vel, masses[None, :]], axis=0)
    targets = jnp.take(sources[0:6], local_index, axis=1)
    total_stars = stars_dev * lax.axis_size("ia") * lax.axis_size("ja")
    gathered = lax.all_gather(targets, ("ia", "ja"), axis=1, tiled=True)
    terms = blocked_sums(sources, gathered, 4096)
    sums = lax.psum_scatter(terms, ("ia", "ja"), scatter_dimension=1, tiled=True)
    sums = sums * (1.0 / total_stars)
    new_acc = sums[0:3]
    new_jerk = sums[3:6]
    step = jnp.take(level_step, local_index)[None, :]
    new_pos, new_vel = correct(
        jnp.take(positions, local_index, axis=1),
        jnp.take(velocities, local_index, axis=1),
        jnp.take(old_acc, local_index, axis=1),
        jnp.take(old_jerk, local_index, axis=1),
        new_acc,
        new_jerk,
        step,
    )
    state = jnp.concatenate([new_pos, new_vel, new_acc, new_jerk], axis=0)
    return jnp.where(live[None, :], state, jnp.float32(0.0))


def solution(mesh):
    in_specs = (
        P(None, ("ia", "ja")),
        P(None, ("ia", "ja")),
        P(None, ("ia", "ja")),
        P(None, ("ia", "ja")),
        P(("ia", "ja")),
        P(("ia", "ja")),
        P(("ia", "ja")),
        P(("ia", "ja"), None),
        P(("ia", "ja")),
    )
    out_specs = P(None, ("ia", "ja"))
    return jax.shard_map(shards, mesh=mesh, in_specs=in_specs, out_specs=out_specs, check_vma=False)
```

profile of v0, /device:TPU:1, one launch (start us, length us, event | category | flops | bytes accessed | tf_op | source)
XLA Modules:
  0.0 1530.8 jit_solution(6249473138673732592)
XLA Ops:
  7.2 0.7 compare_select_fusion.1
  7.9 0.7 compare_and_fusion
  8.6 1.2 fusion.18
  9.9 0.7 multiply_multiply_fusion.2
  10.6 0.8 multiply_add_fusion
  11.7 1.0 gather_fusion
  12.8 0.8 select_bitcast_fusion
  13.7 240.5 %all-gather.2.cloned.1.call-done = f32[6,65536]{0,1:T(8,128)} async-done(((f32[6,512]{0,1:T(8,128)}), f32[6,65536]{0,1:T(8,128)}) %all-gather.2.cloned.1.call-update) | async-done | bytes 1572880 | tf_op jit(solution)/shard_map/all_gather | solution.py:77
  254.2 17.9 %copy.81 = f32[6,16,4096]{2,0,1:T(8,128)S(1)} copy(f32[6,16,4096]{0,2,1:T(8,128)} %bitcast.92) | data formatting | bytes 3145728 | tf_op jit(solution)/shard_map/reshape | solution.py:43
  272.1 618.9 %while.10 = (s32[]{:T(128)}, f32[16,6,4096]{2,1,0:T(8,128)}, f32[3,1536]{1,0:T(4,128)S(1)}, f32[16,6,4096]{2,1,0:T(8,128)S(1)}, f32[1536]{0:T(1024)S(1)}, /*inde...) while((s32[]{:T(128)}, f32[16,6,4096]{2,1,0:T(8,128)}, ...), condition=%wide.region_8.10_spmd, body=%wide.region_1.9_spmd.sunk | while | flops 251633664 | bytes 936157 | solution.py:44
  272.4 37.7 %fusion.38 = (f32[4096]{0:T(1024)S(1)}, f32[4096]{0:T(1024)S(1)}, f32[4096]{0:T(1024)S(1)}, f32[4096]{0:T(1024)S(1)}, f32[4096]{0:T(1024)S(1)}, /*index=5*/f32[4096]{0:T(1024)S(1)}) fusion(f32[4096]{0:T(1024)S(1)} %bitcast.106, f32[1536]{0:T(1024)S(1)} %get-tuple-element.147, f32[4096]{0:T(1024)S(1)} %bitcast.103, f32[1536]{0:T(1024)S(1)} %get-tuple-element.149, ...), kind=kLoop, calls=%fused_computation.27.clone.1 | loop fusion | flops 251633664 | bytes 239616 | tf_op jit(solution)/shard_map/while/body/eval_jaxpr/reduce_sum | solution.py:36
  310.2 0.7 bitcast_dynamic-update-slice_fusion.2
  311.0 37.7 %fusion.38 = (f32[4096]{0:T(1024)S(1)}, f32[4096]{0:T(1024)S(1)}, f32[4096]{0:T(1024)S(1)}, f32[4096]{0:T(1024)S(1)}, f32[4096]{0:T(1024)S(1)}, /*index=5*/f32[4096]{0:T(1024)S(1)}) fusion(f32[4096]{0:T(1024)S(1)} %bitcast.106, f32[1536]{0:T(1024)S(1)} %get-tuple-element.147, f32[4096]{0:T(1024)S(1)} %bitcast.103, f32[1536]{0:T(1024)S(1)} %get-tuple-element.149, ...), kind=kLoop, calls=%fused_computation.27.clone.1 | loop fusion | flops 251633664 | bytes 239616 | tf_op jit(solution)/shard_map/while/body/eval_jaxpr/reduce_sum | solution.py:36
  348.8 0.7 bitcast_dynamic-update-slice_fusion.2
  349.7 37.7 %fusion.38 = (f32[4096]{0:T(1024)S(1)}, f32[4096]{0:T(1024)S(1)}, f32[4096]{0:T(1024)S(1)}, f32[4096]{0:T(1024)S(1)}, f32[4096]{0:T(1024)S(1)}, /*index=5*/f32[4096]{0:T(1024)S(1)}) fusion(f32[4096]{0:T(1024)S(1)} %bitcast.106, f32[1536]{0:T(1024)S(1)} %get-tuple-element.147, f32[4096]{0:T(1024)S(1)} %bitcast.103, f32[1536]{0:T(1024)S(1)} %get-tuple-element.149, ...), kind=kLoop, calls=%fused_computation.27.clone.1 | loop fusion | flops 251633664 | bytes 239616 | tf_op jit(solution)/shard_map/while/body/eval_jaxpr/reduce_sum | solution.py:36
  387.5 0.7 bitcast_dynamic-update-slice_fusion.2
  388.4 37.7 %fusion.38 = (f32[4096]{0:T(1024)S(1)}, f32[4096]{0:T(1024)S(1)}, f32[4096]{0:T(1024)S(1)}, f32[4096]{0:T(1024)S(1)}, f32[4096]{0:T(1024)S(1)}, /*index=5*/f32[4096]{0:T(1024)S(1)}) fusion(f32[4096]{0:T(1024)S(1)} %bitcast.106, f32[1536]{0:T(1024)S(1)} %get-tuple-element.147, f32[4096]{0:T(1024)S(1)} %bitcast.103, f32[1536]{0:T(1024)S(1)} %get-tuple-element.149, ...), kind=kLoop, calls=%fused_computation.27.clone.1 | loop fusion | flops 251633664 | bytes 239616 | tf_op jit(solution)/shard_map/while/body/eval_jaxpr/reduce_sum | solution.py:36
  426.2 0.7 bitcast_dynamic-update-slice_fusion.2
  427.1 37.7 %fusion.38 = (f32[4096]{0:T(1024)S(1)}, f32[4096]{0:T(1024)S(1)}, f32[4096]{0:T(1024)S(1)}, f32[4096]{0:T(1024)S(1)}, f32[4096]{0:T(1024)S(1)}, /*index=5*/f32[4096]{0:T(1024)S(1)}) fusion(f32[4096]{0:T(1024)S(1)} %bitcast.106, f32[1536]{0:T(1024)S(1)} %get-tuple-element.147, f32[4096]{0:T(1024)S(1)} %bitcast.103, f32[1536]{0:T(1024)S(1)} %get-tuple-element.149, ...), kind=kLoop, calls=%fused_computation.27.clone.1 | loop fusion | flops 251633664 | bytes 239616 | tf_op jit(solution)/shard_map/while/body/eval_jaxpr/reduce_sum | solution.py:36
  464.9 0.7 bitcast_dynamic-update-slice_fusion.2
  465.7 37.7 %fusion.38 = (f32[4096]{0:T(1024)S(1)}, f32[4096]{0:T(1024)S(1)}, f32[4096]{0:T(1024)S(1)}, f32[4096]{0:T(1024)S(1)}, f32[4096]{0:T(1024)S(1)}, /*index=5*/f32[4096]{0:T(1024)S(1)}) fusion(f32[4096]{0:T(1024)S(1)} %bitcast.106, f32[1536]{0:T(1024)S(1)} %get-tuple-element.147, f32[4096]{0:T(1024)S(1)} %bitcast.103, f32[1536]{0:T(1024)S(1)} %get-tuple-element.149, ...), kind=kLoop, calls=%fused_computation.27.clone.1 | loop fusion | flops 251633664 | bytes 239616 | tf_op jit(solution)/shard_map/while/body/eval_jaxpr/reduce_sum | solution.py:36
  503.6 0.7 bitcast_dynamic-update-slice_fusion.2
  504.4 37.7 %fusion.38 = (f32[4096]{0:T(1024)S(1)}, f32[4096]{0:T(1024)S(1)}, f32[4096]{0:T(1024)S(1)}, f32[4096]{0:T(1024)S(1)}, f32[4096]{0:T(1024)S(1)}, /*index=5*/f32[4096]{0:T(1024)S(1)}) fusion(f32[4096]{0:T(1024)S(1)} %bitcast.106, f32[1536]{0:T(1024)S(1)} %get-tuple-element.147, f32[4096]{0:T(1024)S(1)} %bitcast.103, f32[1536]{0:T(1024)S(1)} %get-tuple-element.149, ...), kind=kLoop, calls=%fused_computation.27.clone.1 | loop fusion | flops 251633664 | bytes 239616 | tf_op jit(solution)/shard_map/while/body/eval_jaxpr/reduce_sum | solution.py:36
  542.2 0.7 bitcast_dynamic-update-slice_fusion.2
  543.1 37.7 %fusion.38 = (f32[4096]{0:T(1024)S(1)}, f32[4096]{0:T(1024)S(1)}, f32[4096]{0:T(1024)S(1)}, f32[4096]{0:T(1024)S(1)}, f32[4096]{0:T(1024)S(1)}, /*index=5*/f32[4096]{0:T(1024)S(1)}) fusion(f32[4096]{0:T(1024)S(1)} %bitcast.106, f32[1536]{0:T(1024)S(1)} %get-tuple-element.147, f32[4096]{0:T(1024)S(1)} %bitcast.103, f32[1536]{0:T(1024)S(1)} %get-tuple-element.149, ...), kind=kLoop, calls=%fused_computation.27.clone.1 | loop fusion | flops 251633664 | bytes 239616 | tf_op jit(solution)/shard_map/while/body/eval_jaxpr/reduce_sum | solution.py:36
  580.9 0.7 bitcast_dynamic-update-slice_fusion.2
  581.8 37.7 %fusion.38 = (f32[4096]{0:T(1024)S(1)}, f32[4096]{0:T(1024)S(1)}, f32[4096]{0:T(1024)S(1)}, f32[4096]{0:T(1024)S(1)}, f32[4096]{0:T(1024)S(1)}, /*index=5*/f32[4096]{0:T(1024)S(1)}) fusion(f32[4096]{0:T(1024)S(1)} %bitcast.106, f32[1536]{0:T(1024)S(1)} %get-tuple-element.147, f32[4096]{0:T(1024)S(1)} %bitcast.103, f32[1536]{0:T(1024)S(1)} %get-tuple-element.149, ...), kind=kLoop, calls=%fused_computation.27.clone.1 | loop fusion | flops 251633664 | bytes 239616 | tf_op jit(solution)/shard_map/while/body/eval_jaxpr/reduce_sum | solution.py:36
  619.6 0.7 bitcast_dynamic-update-slice_fusion.2
  620.5 37.7 %fusion.38 = (f32[4096]{0:T(1024)S(1)}, f32[4096]{0:T(1024)S(1)}, f32[4096]{0:T(1024)S(1)}, f32[4096]{0:T(1024)S(1)}, f32[4096]{0:T(1024)S(1)}, /*index=5*/f32[4096]{0:T(1024)S(1)}) fusion(f32[4096]{0:T(1024)S(1)} %bitcast.106, f32[1536]{0:T(1024)S(1)} %get-tuple-element.147, f32[4096]{0:T(1024)S(1)} %bitcast.103, f32[1536]{0:T(1024)S(1)} %get-tuple-element.149, ...), kind=kLoop, calls=%fused_computation.27.clone.1 | loop fusion | flops 251633664 | bytes 239616 | tf_op jit(solution)/shard_map/while/body/eval_jaxpr/reduce_sum | solution.py:36
  659.2 37.7 %fusion.38 = (f32[4096]{0:T(1024)S(1)}, f32[4096]{0:T(1024)S(1)}, f32[4096]{0:T(1024)S(1)}, f32[4096]{0:T(1024)S(1)}, f32[4096]{0:T(1024)S(1)}, /*index=5*/f32[4096]{0:T(1024)S(1)}) fusion(f32[4096]{0:T(1024)S(1)} %bitcast.106, f32[1536]{0:T(1024)S(1)} %get-tuple-element.147, f32[4096]{0:T(1024)S(1)} %bitcast.103, f32[1536]{0:T(1024)S(1)} %get-tuple-element.149, ...), kind=kLoop, calls=%fused_computation.27.clone.1 | loop fusion | flops 251633664 | bytes 239616 | tf_op jit(solution)/shard_map/while/body/eval_jaxpr/reduce_sum | solution.py:36
  697.0 0.7 bitcast_dynamic-update-slice_fusion.2
  697.9 37.7 %fusion.38 = (f32[4096]{0:T(1024)S(1)}, f32[4096]{0:T(1024)S(1)}, f32[4096]{0:T(1024)S(1)}, f32[4096]{0:T(1024)S(1)}, f32[4096]{0:T(1024)S(1)}, /*index=5*/f32[4096]{0:T(1024)S(1)}) fusion(f32[4096]{0:T(1024)S(1)} %bitcast.106, f32[1536]{0:T(1024)S(1)} %get-tuple-element.147, f32[4096]{0:T(1024)S(1)} %bitcast.103, f32[1536]{0:T(1024)S(1)} %get-tuple-element.149, ...), kind=kLoop, calls=%fused_computation.27.clone.1 | loop fusion | flops 251633664 | bytes 239616 | tf_op jit(solution)/shard_map/while/body/eval_jaxpr/reduce_sum | solution.py:36
  735.7 0.7 bitcast_dynamic-update-slice_fusion.2
  736.5 37.7 %fusion.38 = (f32[4096]{0:T(1024)S(1)}, f32[4096]{0:T(1024)S(1)}, f32[4096]{0:T(1024)S(1)}, f32[4096]{0:T(1024)S(1)}, f32[4096]{0:T(1024)S(1)}, /*index=5*/f32[4096]{0:T(1024)S(1)}) fusion(f32[4096]{0:T(1024)S(1)} %bitcast.106, f32[1536]{0:T(1024)S(1)} %get-tuple-element.147, f32[4096]{0:T(1024)S(1)} %bitcast.103, f32[1536]{0:T(1024)S(1)} %get-tuple-element.149, ...), kind=kLoop, calls=%fused_computation.27.clone.1 | loop fusion | flops 251633664 | bytes 239616 | tf_op jit(solution)/shard_map/while/body/eval_jaxpr/reduce_sum | solution.py:36
  774.3 0.7 bitcast_dynamic-update-slice_fusion.2
  775.2 37.7 %fusion.38 = (f32[4096]{0:T(1024)S(1)}, f32[4096]{0:T(1024)S(1)}, f32[4096]{0:T(1024)S(1)}, f32[4096]{0:T(1024)S(1)}, f32[4096]{0:T(1024)S(1)}, /*index=5*/f32[4096]{0:T(1024)S(1)}) fusion(f32[4096]{0:T(1024)S(1)} %bitcast.106, f32[1536]{0:T(1024)S(1)} %get-tuple-element.147, f32[4096]{0:T(1024)S(1)} %bitcast.103, f32[1536]{0:T(1024)S(1)} %get-tuple-element.149, ...), kind=kLoop, calls=%fused_computation.27.clone.1 | loop fusion | flops 251633664 | bytes 239616 | tf_op jit(solution)/shard_map/while/body/eval_jaxpr/reduce_sum | solution.py:36
  813.0 0.7 bitcast_dynamic-update-slice_fusion.2
  813.9 37.7 %fusion.38 = (f32[4096]{0:T(1024)S(1)}, f32[4096]{0:T(1024)S(1)}, f32[4096]{0:T(1024)S(1)}, f32[4096]{0:T(1024)S(1)}, f32[4096]{0:T(1024)S(1)}, /*index=5*/f32[4096]{0:T(1024)S(1)}) fusion(f32[4096]{0:T(1024)S(1)} %bitcast.106, f32[1536]{0:T(1024)S(1)} %get-tuple-element.147, f32[4096]{0:T(1024)S(1)} %bitcast.103, f32[1536]{0:T(1024)S(1)} %get-tuple-element.149, ...), kind=kLoop, calls=%fused_computation.27.clone.1 | loop fusion | flops 251633664 | bytes 239616 | tf_op jit(solution)/shard_map/while/body/eval_jaxpr/reduce_sum | solution.py:36
  851.7 0.7 bitcast_dynamic-update-slice_fusion.2
  852.6 37.7 %fusion.38 = (f32[4096]{0:T(1024)S(1)}, f32[4096]{0:T(1024)S(1)}, f32[4096]{0:T(1024)S(1)}, f32[4096]{0:T(1024)S(1)}, f32[4096]{0:T(1024)S(1)}, /*index=5*/f32[4096]{0:T(1024)S(1)}) fusion(f32[4096]{0:T(1024)S(1)} %bitcast.106, f32[1536]{0:T(1024)S(1)} %get-tuple-element.147, f32[4096]{0:T(1024)S(1)} %bitcast.103, f32[1536]{0:T(1024)S(1)} %get-tuple-element.149, ...), kind=kLoop, calls=%fused_computation.27.clone.1 | loop fusion | flops 251633664 | bytes 239616 | tf_op jit(solution)/shard_map/while/body/eval_jaxpr/reduce_sum | solution.py:36
  890.4 0.7 bitcast_dynamic-update-slice_fusion.2
  892.3 3.1 gather_fusion.1
  895.5 1.0 gather_fusion.2
  896.7 1.0 gather_fusion.3
  897.8 1.0 gather_fusion.4
  899.0 1.0 gather_fusion.5
  900.1 622.5 %reduce-scatter.2.cloned.1.call-done = f32[6,512]{1,0:T(8,128)} async-done(((f32[6,65536]{1,0:T(8,128)}), f32[6,512]{1,0:T(8,128)}) %reduce-scatter.2.cloned.1.call-update) | async-done | bytes 12304 | tf_op jit(solution)/shard_map/reduce_scatter | solution.py:79
  1522.6 0.7 broadcast_multiply_fusion
  (84 shorter events, 8.9 us)
Async XLA Ops:
  6.5 265.5 %copy-start.5 = (f32[1536]{0:T(1024)S(1)}, f32[1536]{0:T(1024)}, u32[]{:S(2)}) copy-start(f32[1536]{0:T(1024)} %param.17) | copy-start | bytes 18436
  6.5 247.6 %all-gather.2.cloned.1.call-start = ((), (), s32[]{:S(2)}) async-start(), calls=%async_computation.1 | async-start | bytes 33816576 | tf_op jit(solution)/shard_map/all_gather | solution.py:77
  13.6 1509.0 %reduce-scatter.2.cloned.1.call-start = ((), (), s32[]{:S(2)}) async-start(), calls=%async_computation.2 | async-start | bytes 2113536 | tf_op jit(solution)/shard_map/reduce_scatter | solution.py:79
  272.1 619.0 %copy-start = (f32[3,1536]{1,0:T(4,128)S(1)}, f32[3,1536]{1,0:T(4,128)}, u32[]{:S(2)}) copy-start(f32[3,1536]{1,0:T(4,128)} %param.13) | copy-start | bytes 55300
  272.1 619.3 %copy-start.1 = (f32[3,1536]{1,0:T(4,128)S(1)}, f32[3,1536]{1,0:T(4,128)}, u32[]{:S(2)}) copy-start(f32[3,1536]{1,0:T(4,128)} %param.14) | copy-start | bytes 55300
  272.1 619.6 %copy-start.2 = (f32[3,1536]{1,0:T(4,128)S(1)}, f32[3,1536]{1,0:T(4,128)}, u32[]{:S(2)}) copy-start(f32[3,1536]{1,0:T(4,128)} %param.15) | copy-start | bytes 55300
  272.1 619.9 %copy-start.3 = (f32[3,1536]{1,0:T(4,128)S(1)}, f32[3,1536]{1,0:T(4,128)}, u32[]{:S(2)}) copy-start(f32[3,1536]{1,0:T(4,128)} %param.16) | copy-start | bytes 55300
  272.1 623.3 %copy-start.4 = (s32[1,512]{1,0:T(1,128)S(1)}, s32[1,512]{1,0:T(1,128)}, u32[]{:S(2)}) copy-start(s32[1,512]{1,0:T(1,128)} %param.20) | copy-start | bytes 6148
Sparse Core Ops, SparseCore 0:
  13.8 240.3 all-gather.1
  891.2 631.3 reduce-scatter.1
where the time goes:
time: 1540 us; the launch traced here: 1530 us
  waiting for transfers between devices  863 us (56%)
  other arithmetic  609 us (40%)
  local copies, waits for them, and re-layouts  44.3 us (3%)
    reduce_scatter x1, waiting for transfers between devices, shards(): lax.psum_scatter(terms, ('ia', 'ja'), scatter_dimension=1, tiled=True)  622 us
    reduce_sum x16, other arithmetic, pair_sums(): jnp.sum((drift_z - radial * gap_z) * weighted, axis=0)  602 us
    all_gather x1, waiting for transfers between devices, shards(): gathered = lax.all_gather(targets, ('ia', 'ja'), axis=1, tiled=True)  240 us
  transfers between devices with their start and end apart: 2, of which 2 were waited for; matrix products, arithmetic and copies ran while one was open for 1% of the time, Pallas kernels for 0%

commit v1 on v0

v1 whole, which is shorter than its diff:
```python
import functools

import jax
import jax.numpy as jnp
from jax import lax
from jax.experimental import pallas as pl
from jax.experimental.pallas import tpu as pltpu
from jax.sharding import PartitionSpec as P

MESH = pl.DeviceIdType.MESH
soften = 0.01
f32 = jnp.float32
bf16 = jnp.bfloat16

STARS = 1536
SLOTS = 512
OWNERS = 128
BLOCK = 256
VMEM_LIMIT = 56 * 2**20


def vmem():
    return pl.BlockSpec(memory_space=pltpu.VMEM)


def smem():
    return pl.BlockSpec(memory_space=pltpu.SMEM)


def split3(x):
    a = x.astype(bf16).astype(f32)
    rest = x - a
    b = rest.astype(bf16).astype(f32)
    return a, b, rest - b


def coords():
    ia, ja = lax.axis_index("ia"), lax.axis_index("ja")
    return ia // 2, ia % 2, ja // 4, (ja // 2) % 2, ja % 2


def device(z, xh, y, xl, core):
    return (z * 2 + xh, y * 4 + xl * 2 + core)


def peers():
    z, xh, y, xl, core = coords()
    x = xh * 2 + xl
    across = device(z, xh, y, xl, 1 - core)
    along_x = [device(z, ((x + d) % 4) // 2, y, ((x + d) % 4) % 2, core) for d in (1, 2, 3)]
    along_y = [device(z, xh, (y + d) % 4, xl, core) for d in (1, 2, 3)]
    along_z = [device((z + d) % 4, xh, y, xl, core) for d in (1, 2, 3)]
    return across, along_x, along_y, along_z


def greet():
    across, along_x, along_y, along_z = peers()
    barrier = pltpu.get_barrier_semaphore()
    for peer in [across] + along_x + along_y + along_z:
        pl.semaphore_signal(barrier, inc=1, device_id=peer, device_id_type=MESH)
    return barrier


def predict(d, step):
    tau_sq = 0.5 * step * step
    tau_cube = step * step * step / 6.0
    pos = d[0:3] + step * d[3:6] + tau_sq * d[6:9] + tau_cube * d[9:12]
    vel = d[3:6] + step * d[6:9] + tau_sq * d[9:12]
    return pos, vel


def gather_kernel(
    pos_ref, vel_ref, acc_ref, jerk_ref, mass_ref, elapsed_ref, levels_ref, index_ref, count_ref,
    all_ref, start_ref, src_ref,
    state, send_sem, recv_sem,
):
    barrier = greet()
    z, xh, y, xl, core = coords()
    across, along_x, along_y, along_z = peers()

    state[...] = jnp.zeros_like(state)
    state[0:3] = pos_ref[...]
    state[3:6] = vel_ref[...]
    state[6:9] = acc_ref[...]
    state[9:12] = jerk_ref[...]
    levels = levels_ref[...]
    step = jnp.where(
        levels == 0, 0.5, jnp.where(levels == 1, 0.25, jnp.where(levels == 2, 0.125, 0.0625))
    ).astype(f32)
    state[12:13] = step

    pick = (lax.broadcasted_iota(jnp.int32, (STARS, SLOTS), 0) == index_ref[...]).astype(f32)
    pick = pick.astype(bf16)
    parts = jnp.concatenate(split3(state[...]), axis=0).astype(bf16)
    rows = jnp.dot(parts, pick, preferred_element_type=f32)
    start = (rows[0:16] + rows[16:32]) + rows[32:48]
    start_ref[...] = start
    pred_pos, pred_vel = predict(start, start[12:13])
    counts = jnp.full((2, SLOTS), count_ref[0], jnp.int32).astype(f32)
    all_ref[z, xh, y, xl, core] = jnp.concatenate([pred_pos, pred_vel, counts], axis=0)

    pl.semaphore_wait(barrier, 10)

    def copies(phase, block, targets):
        out = []
        for k, target in enumerate(targets):
            copy = pltpu.make_async_remote_copy(
                src_ref=block, dst_ref=block, send_sem=send_sem.at[phase, k],
                recv_sem=recv_sem.at[phase, k], device_id=target, device_id_type=MESH,
            )
            copy.start()
            out.append(copy)
        return out

    along_x = copies(0, all_ref.at[z, xh, y, xl, core], along_x)

    live = lax.broadcasted_iota(jnp.int32, (8, SLOTS), 1) < count_ref[0]
    live = live.astype(f32).astype(bf16)
    chosen = lax.dot_general(
        live, pick, (((1,), (1,)), ((), ())), preferred_element_type=f32
    )[0:1]
    interval = jnp.where(chosen > 0.5, step, elapsed_ref[...])
    src_pos, src_vel = predict(state[...], interval)
    mass = mass_ref[...]
    src_ref[...] = jnp.concatenate([src_pos, src_vel, mass, jnp.ones_like(mass)], axis=0)

    for c in along_x:
        c.wait_recv()
    along_y = copies(1, all_ref.at[z, :, y, :, core], along_y)
    for c in along_y:
        c.wait_recv()
    along_z = copies(2, all_ref.at[z, :, :, :, core], along_z)
    over = copies(3, all_ref.at[z, :, :, :, core], [across])
    for d in (1, 2, 3):
        along_z[d - 1].wait_recv()
        over += copies(3 + d, all_ref.at[(z - d + 4) % 4, :, :, :, core], [across])
    for c in over:
        c.wait_recv()
    for c in along_x + along_y + along_z + over:
        c.wait_send()


def pair_kernel(all_ref, src_ref, count_ref, out_ref, comp, sums, hq, hr, fw, fb):
    lane = lax.broadcasted_iota(jnp.int32, (8, 128), 1)

    def pack(o, offset):
        shift = offset % 128
        base = pl.multiple_of(offset - shift, 128)
        x = jnp.concatenate([all_ref[o], jnp.zeros((8, 128), f32)], axis=1)
        x = pltpu.roll(x, shift, 1)
        first = pl.ds(base, 128)
        comp[:, first] = jnp.where(lane < shift, comp[:, first], x[:, 0:128])
        comp[:, pl.ds(base + 128, SLOTS)] = x[:, 128:]
        return offset + count_ref[o]

    total = lax.fori_loop(0, OWNERS, pack, jnp.int32(0))

    src = src_ref[...]
    row = lax.broadcasted_iota(jnp.int32, (8, 1), 0)
    centre = jnp.sum(src, axis=1, keepdims=True) * (1.0 / STARS)
    centre = jnp.where(row < 6, jnp.floor(centre * 64.0 + 0.5) * (1.0 / 64.0), 0.0)
    src = src - centre
    mass = src[6:7]
    s_sq = src[0:1] * src[0:1] + src[1:2] * src[1:2] + src[2:3] * src[2:3]
    s_rv = src[0:1] * src[3:4] + src[1:2] * src[4:5] + src[2:3] * src[5:6]
    zero = jnp.zeros_like(s_sq)
    plain = split3(jnp.concatenate([src[0:3] * -2.0, zero, zero, zero, zero, zero], axis=0))
    swapped = split3(jnp.concatenate([-src[3:6], -src[0:3], zero, zero], axis=0))
    unit_q = (row == 6).astype(f32)
    unit_r = (row == 7).astype(f32)
    sq_parts = jnp.concatenate(split3(s_sq) + (zero,) * 5, axis=0)
    rv_parts = jnp.concatenate(split3(s_rv) + (zero,) * 5, axis=0)
    fill = jnp.zeros((72, STARS), f32)
    hq_rows = jnp.concatenate(
        [plain[0] + unit_q, plain[1], plain[0] + unit_q, plain[1], plain[2], plain[0] + unit_q,
         sq_parts, fill], axis=0)
    hr_rows = jnp.concatenate(
        [swapped[0] + unit_r, swapped[1], swapped[0] + unit_r, swapped[1], swapped[2],
         swapped[0] + unit_r, rv_parts, fill], axis=0)
    hq[...] = hq_rows.T.astype(bf16)
    hr[...] = hr_rows.T.astype(bf16)
    weights = jnp.concatenate([src[0:6], zero + 1.0, zero], axis=0) * mass
    pad8 = jnp.zeros((8, STARS), f32)
    fw[...] = jnp.concatenate(split3(weights) + (pad8,), axis=0).astype(bf16)
    weights = jnp.where((row < 3) | (row == 6), weights, 0.0)
    fb[...] = jnp.concatenate(split3(weights) + (pad8,), axis=0).astype(bf16)

    def block(i, carry):
        cols = pl.ds(pl.multiple_of(i * BLOCK, BLOCK), BLOCK)
        t = comp[:, cols] - centre
        t_sq = t[0:1] * t[0:1] + t[1:2] * t[1:2] + t[2:3] * t[2:3] + soften
        t_rv = t[0:1] * t[3:4] + t[1:2] * t[4:5] + t[2:3] * t[5:6]
        p0, p1, p2 = split3(jnp.concatenate([t[0:6], t_sq, t_rv], axis=0))
        ones = jnp.ones((8, BLOCK), f32)
        g = jnp.concatenate(
            [p0, p0, p1, p1, p0, p2, ones, jnp.zeros((72, BLOCK), f32)], axis=0
        ).astype(bf16)
        q = jnp.dot(hq[...], g, preferred_element_type=f32)
        rv = jnp.dot(hr[...], g, preferred_element_type=f32)
        inv = lax.rsqrt(q)
        inv2 = inv * inv
        w = inv2 * inv
        b = w * inv2 * rv
        w_hi = w.astype(bf16)
        b_hi = b.astype(bf16)
        w_lo = (w - w_hi.astype(f32)).astype(bf16)
        b_lo = (b - b_hi.astype(f32)).astype(bf16)
        sw = jnp.dot(fw[...], w_hi, preferred_element_type=f32)
        sb = jnp.dot(fb[...], b_hi, preferred_element_type=f32)
        swl = jnp.dot(fw[0:16], w_lo, preferred_element_type=f32)
        sbl = jnp.dot(fb[0:16], b_lo, preferred_element_type=f32)
        sw = sw[0:8] + (sw[8:16] + (sw[16:24] + (swl[0:8] + swl[8:16])))
        sb = sb[0:8] + (sb[8:16] + (sb[16:24] + (sbl[0:8] + sbl[8:16])))
        rw = sw - t * sw[6:7]
        rb = sb - t * sb[6:7]
        rb = pltpu.roll(rb, 3, 0)
        sums[:, cols] = rw - jnp.where((row >= 3) & (row < 6), 3.0 * rb, 0.0)
        return carry

    lax.fori_loop(0, (total + BLOCK - 1) // BLOCK, block, 0)

    def unpack(o, offset):
        shift = offset % 128
        base = pl.multiple_of(offset - shift, 128)
        x = sums[:, pl.ds(base, SLOTS + 128)]
        x = pltpu.roll(x, (SLOTS + 128) - shift, 1)
        out_ref[o] = x[:, 0:SLOTS]
        return offset + count_ref[o]

    lax.fori_loop(0, OWNERS, unpack, jnp.int32(0))


def reduce_kernel(
    part_ref, start_ref, count_ref, out_ref,
    got_core, got_z, got_y, got_x, sum_z, sum_y, send_sem, recv_sem,
):
    barrier = greet()
    z, xh, y, xl, core = coords()
    across, along_x, along_y, along_z = peers()
    pl.semaphore_wait(barrier, 10)
    sent = []

    def copy(phase, k, src, dst, target):
        c = pltpu.make_async_remote_copy(
            src_ref=src, dst_ref=dst, send_sem=send_sem.at[phase, k],
            recv_sem=recv_sem.at[phase, k], device_id=target, device_id_type=MESH,
        )
        c.start()
        sent.append(c)
        return c

    over = []
    for d in (1, 2, 3, 4):
        zt = (z + d) % 4
        over.append(copy(0, d - 1, part_ref.at[zt, :, :, :, 1 - core], got_core.at[d - 1], across))
    from_z = []
    for d in (1, 2, 3, 4):
        zt = (z + d) % 4
        over[d - 1].wait_recv()
        sum_z[d - 1] = part_ref[zt, :, :, :, core] + got_core[d - 1]
        if d < 4:
            from_z.append(copy(1, d - 1, sum_z.at[d - 1], got_z.at[d - 1], along_z[d - 1]))
    for c in from_z:
        c.wait_recv()
    sum_z[3] = sum_z[3] + (got_z[0] + got_z[1] + got_z[2])
    from_y = []
    for d in (1, 2, 3):
        yt = (y + d) % 4
        from_y.append(copy(2, d - 1, sum_z.at[3, :, yt], got_y.at[d - 1], along_y[d - 1]))
    for c in from_y:
        c.wait_recv()
    sum_y[...] = sum_z[3, :, y] + (got_y[0] + got_y[1] + got_y[2])
    from_x = []
    x = xh * 2 + xl
    for d in (1, 2, 3):
        xt = (x + d) % 4
        from_x.append(copy(3, d - 1, sum_y.at[xt // 2, xt % 2], got_x.at[d - 1], along_x[d - 1]))
    for c in from_x:
        c.wait_recv()
    total = sum_y[xh, xl] + (got_x[0] + got_x[1] + got_x[2])

    total = total * (1.0 / (STARS * OWNERS))
    start = start_ref[...]
    step = start[12:13]
    acc0, jerk0 = start[6:9], start[9:12]
    acc1, jerk1 = total[0:3], total[3:6]
    vel1 = start[3:6] + (acc0 + acc1) * step / 2.0 + (jerk0 - jerk1) * step * step / 12.0
    pos1 = start[0:3] + (start[3:6] + vel1) * step / 2.0 + (acc0 - acc1) * step * step / 12.0
    state = jnp.concatenate([pos1, vel1, acc1, jerk1], axis=0)
    live = lax.broadcasted_iota(jnp.int32, (12, SLOTS), 1) < count_ref[0]
    out_ref[...] = jnp.where(live, state, 0.0)
    for c in sent:
        c.wait_send()


def shards(
    positions, velocities, old_acc, old_jerk, masses, elapsed, levels, active_index, active_count
):
    every, start, src = pl.pallas_call(
        gather_kernel,
        out_shape=(
            jax.ShapeDtypeStruct((4, 2, 4, 2, 2, 8, SLOTS), f32),
            jax.ShapeDtypeStruct((16, SLOTS), f32),
            jax.ShapeDtypeStruct((8, STARS), f32),
        ),
        in_specs=[vmem()] * 8 + [smem()],
        out_specs=(vmem(), vmem(), vmem()),
        scratch_shapes=[
            pltpu.VMEM((16, STARS), f32),
            pltpu.SemaphoreType.DMA((7, 3)),
            pltpu.SemaphoreType.DMA((7, 3)),
        ],
        compiler_params=pltpu.CompilerParams(
            collective_id=0, has_side_effects=True, vmem_limit_bytes=VMEM_LIMIT
        ),
        name="predict_gather",
    )(
        positions, velocities, old_acc, old_jerk, masses.reshape(1, STARS),
        elapsed.reshape(1, STARS), levels.reshape(1, STARS), active_index, active_count,
    )
    every = every.reshape(OWNERS, 8, SLOTS)
    counts = every[:, 6, 0].astype(jnp.int32)
    parts = pl.pallas_call(
        pair_kernel,
        out_shape=jax.ShapeDtypeStruct((OWNERS, 8, SLOTS), f32),
        in_specs=[vmem(), vmem(), smem()],
        out_specs=vmem(),
        scratch_shapes=[
            pltpu.VMEM((8, OWNERS * SLOTS + SLOTS + 128), f32),
            pltpu.VMEM((8, OWNERS * SLOTS + SLOTS + 128), f32),
            pltpu.VMEM((STARS, 128), bf16),
            pltpu.VMEM((STARS, 128), bf16),
            pltpu.VMEM((32, STARS), bf16),
            pltpu.VMEM((32, STARS), bf16),
        ],
        compiler_params=pltpu.CompilerParams(vmem_limit_bytes=VMEM_LIMIT),
        name="pair_sums",
    )(every, src, counts)
    return pl.pallas_call(
        reduce_kernel,
        out_shape=jax.ShapeDtypeStruct((12, SLOTS), f32),
        in_specs=[vmem(), vmem(), smem()],
        out_specs=vmem(),
        scratch_shapes=[
            pltpu.VMEM((4, 2, 4, 2, 8, SLOTS), f32),
            pltpu.VMEM((3, 2, 4, 2, 8, SLOTS), f32),
            pltpu.VMEM((3, 2, 2, 8, SLOTS), f32),
            pltpu.VMEM((3, 8, SLOTS), f32),
            pltpu.VMEM((4, 2, 4, 2, 8, SLOTS), f32),
            pltpu.VMEM((2, 2, 8, SLOTS), f32),
            pltpu.SemaphoreType.DMA((4, 4)),
            pltpu.SemaphoreType.DMA((4, 4)),
        ],
        compiler_params=pltpu.CompilerParams(
            collective_id=1, has_side_effects=True, vmem_limit_bytes=VMEM_LIMIT
        ),
        name="reduce_correct",
    )(parts.reshape(4, 2, 4, 2, 2, 8, SLOTS), start, active_count)


def solution(mesh):
    every = ("ia", "ja")
    in_specs = (
        P(None, every), P(None, every), P(None, every), P(None, every),
        P(every), P(every), P(every), P(every, None), P(every),
    )
    return jax.shard_map(
        shards, mesh=mesh, in_specs=in_specs, out_specs=P(None, every), check_vma=False
    )
```

time: 1540 us -> 218 us (0.14)
  waiting for transfers between devices: 863 us -> 0 us
  other arithmetic: 609 us -> 3.91 us
  Pallas kernels: 0 us -> 207 us
  local copies, waits for them, and re-layouts: 44.3 us -> 5.26 us
    reduce_scatter x1 -> x0, waiting for transfers between devices: 622 us -> none  [shards(): lax.psum_scatter(terms, ('ia', 'ja'), scatter_dimension=1, tiled=True)]
    reduce_sum x16 -> x0, other arithmetic: 602 us -> none  [pair_sums(): jnp.sum((drift_z - radial * gap_z) * weighted, axis=0)]
    all_gather x1 -> x0, waiting for transfers between devices: 240 us -> none  [shards(): gathered = lax.all_gather(targets, ('ia', 'ja'), axis=1, tiled=True)]
    pallas_call x0 -> x3, Pallas kernels: none -> 207 us  [the longest x1 148 us: shards(): pl.pallas_call(pair_kernel, out_shape=jax.ShapeDtypeStruct((OWNERS, 8, SL...]
  transfers between devices with their start and end apart: 2 -> 0, of which waited for: 2 -> 0; matrix products, arithmetic and copies ran while one was open for 1% -> 0% of each run, Pallas kernels for 0% -> 0%
where the time goes in v1:
time: 218 us; the launch traced here: 217 us
  Pallas kernels  207 us (95%)
  local copies, waits for them, and re-layouts  5.26 us (2%)
  other arithmetic  3.91 us (2%)
    pallas_call x1, Pallas kernels, shards(): pl.pallas_call(pair_kernel, out_shape=jax.ShapeDtypeStruct((OWNERS, 8, SL...  148 us
    pallas_call x1, Pallas kernels, shards(): pl.pallas_call(gather_kernel, out_shape=(jax.ShapeDtypeStruct((4, 2, 4, 2...  32.1 us
    pallas_call x1, Pallas kernels, shards(): pl.pallas_call(reduce_kernel, out_shape=jax.ShapeDtypeStruct((12, SLOTS),...  27 us

profile of v1, /device:TPU:1, one launch (start us, length us, event | category | flops | bytes accessed | tf_op | source)
XLA Modules:
  0.0 216.5 jit_solution(15651993069979382462)
XLA Ops:
  0.7 1.3 reshape.16.mass_ref
  1.9 1.3 reshape.17.elapsed_ref
  3.2 1.3 reshape.18.levels_ref
  4.5 32.1 %predict_gather.1 = (f32[4,2,4,2,2,8,512]{6,5,4,3,2,1,0:T(8,128)}, f32[16,512]{1,0:T(8,128)}, f32[8,1536]{1,0:T(8,128)}) custom-call(f32[3,1536]{1,0:T(4,128)} %pos_ref.1, f32[3,1536]{1,0:T(4,128)} %vel_ref.1, f32[3,1536]{1,0:T(4,128)} %acc_ref.1, f32[3,1536]{1,0:T(4,128)} %jerk_ref.1, f32[1,1536]{1,0:T(1,128)} %reshape.16.mass_ref, ...), custom_call_target="tpu_custom_call" | custom-call | tf_op jit(solution)/shard_map/predict_gather/pallas_call | solution.py:299
  36.6 3.9 %fusion.count_ref = s32[128]{0:T(128)} fusion(f32[128,8,512]{2,1,0:T(8,128)} %bitcast.3), kind=kLoop, calls=%fused_computation.1 | loop fusion | flops 128 | bytes 1024 | tf_op jit(solution)/shard_map/convert_element_type | solution.py:322
  40.5 147.7 %pair_sums.1 = f32[128,8,512]{2,1,0:T(8,128)} custom-call(f32[128,8,512]{2,1,0:T(8,128)} %bitcast.4, f32[8,1536]{1,0:T(8,128)} %get-tuple-element.9.src_ref, s32[128]{0:T(128)} %fusion.count_ref), custom_call_target="tpu_custom_call" | custom-call | tf_op jit(solution)/shard_map/pair_sums/pallas_call | solution.py:323
  188.2 27.0 %reduce_correct.1 = f32[12,512]{1,0:T(8,128)} custom-call(f32[4,2,4,2,2,8,512]{6,5,4,3,2,1,0:T(8,128)} %bitcast.2, f32[16,512]{1,0:T(8,128)} %get-tuple-element.10.start_ref, s32[1]{0:T(128)S(6)} %copy.11.count_ref), custom_call_target="tpu_custom_call" | custom-call | tf_op jit(solution)/shard_map/reduce_correct/pallas_call | solution.py:339
  215.2 1.4 copy.12

commit v2 on v1

v2 whole, which is shorter than its diff:
```python
import jax
import jax.numpy as jnp
from jax import lax
from jax.experimental import pallas as pl
from jax.experimental.pallas import tpu as pltpu
from jax.sharding import PartitionSpec as P

MESH = pl.DeviceIdType.MESH
soften = 0.01
f32 = jnp.float32
bf16 = jnp.bfloat16
f8 = jnp.float8_e4m3fn

STARS = 1536
SLOTS = 512
OWNERS = 128
BLOCK = 256
CHUNK = 768
ROOM = OWNERS * SLOTS + SLOTS + 128
VMEM_LIMIT = 56 * 2**20
PAIRS = 3
GATHER_ORDER = ("xyz", "yzx", "zxy")
REDUCE_ORDER = (
    ("zyx", (2, 4, 2), (2, 2), lambda r, j: r.at[:, j], lambda r, j: r.at[j // 2, j % 2]),
    ("xzy", (4, 4), (4,), lambda r, j: r.at[j], lambda r, j: r.at[j]),
    ("yxz", (4, 2, 2), (4,), lambda r, j: r.at[:, j // 2, j % 2], lambda r, j: r.at[j]),
)
PLACES = (4, 2, 4, 2, 2, 8, 128)
POS_SCALE = 2.0**-2
VEL_SCALE = 2.0**-8
W_SCALE = 2.0**6


def vmem():
    return pl.BlockSpec(memory_space=pltpu.VMEM)


def smem():
    return pl.BlockSpec(memory_space=pltpu.SMEM)


def split3(x):
    a = x.astype(bf16).astype(f32)
    rest = x - a
    b = rest.astype(bf16).astype(f32)
    return a, b, rest - b


def place():
    ia, ja = lax.axis_index("ia"), lax.axis_index("ja")
    return {"z": ia // 2, "x": (ia % 2) * 2 + (ja // 2) % 2, "y": ja // 4}, ja % 2


def device(at, core):
    return (at["z"] * 2 + at["x"] // 2, at["y"] * 4 + (at["x"] % 2) * 2 + core)


def along(me, core, axis, d):
    return device({**me, axis: (me[axis] + d) % 4}, core)


def view(ref, at, core):
    xh, xl = (slice(None),) * 2 if at["x"] is None else (at["x"] // 2, at["x"] % 2)
    z = slice(None) if at["z"] is None else at["z"]
    y = slice(None) if at["y"] is None else at["y"]
    return ref.at[z, xh, y, xl, core]


def greet():
    me, core = place()
    barrier = pltpu.get_barrier_semaphore()
    peers = [along(me, core, axis, d) for axis in "xyz" for d in (1, 2, 3)]
    for peer in [device(me, 1 - core)] + peers:
        pl.semaphore_signal(barrier, inc=1, device_id=peer, device_id_type=MESH)
    return barrier


def predict(d, step):
    tau_sq = 0.5 * step * step
    tau_cube = step * step * step / 6.0
    pos = d[0:3] + step * d[3:6] + tau_sq * d[6:9] + tau_cube * d[9:12]
    vel = d[3:6] + step * d[6:9] + tau_sq * d[9:12]
    return pos, vel


def flat(ref):
    return jnp.concatenate([ref[i:i + 1, :] for i in range(STARS // 128)], axis=1)


def fold(rows):
    return jnp.concatenate([rows[:, 128 * t:128 * (t + 1)] for t in range(4)], axis=0)


def unfold(blocks):
    return jnp.concatenate(
        [jnp.concatenate([b[2 * t:2 * t + 2] for b in blocks], axis=0) for t in range(4)], axis=1
    )


def gather_kernel(
    pos_ref, vel_ref, acc_ref, jerk_ref, mass_ref, elapsed_ref, levels_ref, index_ref, count_ref,
    all0, all1, all2, start_ref, hq_ref, hr_ref, fw_ref, f8_ref, centre_ref,
    state, send_sem, recv_sem,
):
    every = (all0, all1, all2)
    barrier = greet()
    me, core = place()
    started = []

    def send(p, phase, k, block, target):
        c = pltpu.make_async_remote_copy(
            src_ref=block, dst_ref=block, send_sem=send_sem.at[p, phase, k],
            recv_sem=recv_sem.at[p, phase, k], device_id=target, device_id_type=MESH,
        )
        c.start()
        started.append(c)
        return c

    state[...] = jnp.zeros_like(state)
    state[0:3] = pos_ref[...]
    state[3:6] = vel_ref[...]
    state[6:9] = acc_ref[...]
    state[9:12] = jerk_ref[...]
    levels = flat(levels_ref)
    step = jnp.where(
        levels == 0, 0.5, jnp.where(levels == 1, 0.25, jnp.where(levels == 2, 0.125, 0.0625))
    ).astype(f32)
    state[12:13] = step

    pick = (lax.broadcasted_iota(jnp.int32, (STARS, SLOTS), 0) == index_ref[...]).astype(f32)
    pick = pick.astype(bf16)
    parts = jnp.concatenate(split3(state[...]), axis=0).astype(bf16)
    rows = jnp.dot(parts, pick, preferred_element_type=f32)
    start = (rows[0:16] + rows[16:32]) + rows[32:48]
    start_ref[...] = start
    target = jnp.concatenate(predict(start, start[12:13]), axis=0)
    live = lax.broadcasted_iota(jnp.int32, (8, SLOTS), 1) < count_ref[0]
    view(all0, me, core)[...] = fold(jnp.where(live[0:2], target[0:2], 1e30))
    view(all1, me, core)[...] = fold(target[2:4])
    view(all2, me, core)[...] = fold(target[4:6])

    pl.semaphore_wait(barrier, 10)

    have = [dict(me) for _ in range(PAIRS)]
    flight = [[] for _ in range(PAIRS)]

    def begin(phase):
        for p in range(PAIRS):
            axis = GATHER_ORDER[p][phase]
            flight[p] = [
                send(p, phase, d - 1, view(every[p], have[p], core), along(me, core, axis, d))
                for d in (1, 2, 3)
            ]

    def finish(phase):
        for p in range(PAIRS):
            for c in flight[p]:
                c.wait_recv()
            have[p][GATHER_ORDER[p][phase]] = None

    begin(0)
    chosen = lax.dot_general(
        live.astype(f32).astype(bf16), pick, (((1,), (1,)), ((), ())),
        preferred_element_type=f32,
    )[0:1]
    interval = jnp.where(chosen > 0.5, step, flat(elapsed_ref))
    src = jnp.concatenate(predict(state[...], interval), axis=0)
    finish(0)
    begin(1)

    centre = jnp.sum(src, axis=1, keepdims=True) * (1.0 / STARS)
    centre = jnp.floor(centre * 64.0 + 0.5) * (1.0 / 64.0)
    src = src - centre
    centre = jnp.concatenate([centre, jnp.zeros((2, 1), f32)], axis=0)
    centre_ref[...] = jnp.broadcast_to(centre, (8, 128))
    zero = jnp.zeros((1, STARS), f32)
    weights = jnp.concatenate([src, zero + 1.0, zero], axis=0) * flat(mass_ref)
    pos, vel = src[0:3] * POS_SCALE, src[3:6] * VEL_SCALE
    row = lax.broadcasted_iota(jnp.int32, (8, 1), 0)

    def factors(own, square, unit):
        a, b, c = split3(jnp.concatenate([own, zero, zero], axis=0))
        a = a + (row == unit).astype(f32)
        s = jnp.concatenate(split3(square) + (zero,) * 5, axis=0)
        fill = jnp.zeros((72, STARS), f32)
        return jnp.concatenate([a, b, a, b, c, a, s, fill], axis=0).T.astype(bf16)

    square = pos[0:1] * pos[0:1] + pos[1:2] * pos[1:2] + pos[2:3] * pos[2:3]
    hq_ref[...] = factors(jnp.concatenate([pos * -2.0, zero, zero, zero], axis=0), square, 6)
    finish(1)
    begin(2)
    over = [
        [send(p, 3, 0, view(every[p], have[p], core), device(me, 1 - core))]
        for p in range(PAIRS)
    ]
    product = pos[0:1] * vel[0:1] + pos[1:2] * vel[1:2] + pos[2:3] * vel[2:3]
    hr_ref[...] = factors(jnp.concatenate([-vel, -pos], axis=0), product, 7)
    fill = jnp.zeros((8, STARS), f32)
    fw_ref[...] = jnp.concatenate(split3(weights) + (fill,), axis=0).astype(bf16)
    high = weights.astype(f8).astype(f32)
    f8_ref[...] = jnp.concatenate([high, weights - high, fill, fill], axis=0).astype(f8)

    for d in (1, 2, 3):
        for p in range(PAIRS):
            axis = GATHER_ORDER[p][2]
            flight[p][d - 1].wait_recv()
            came = {**have[p], axis: (me[axis] - d + 4) % 4}
            over[p].append(send(p, 3, d, view(every[p], came, core), device(me, 1 - core)))
    for p in range(PAIRS):
        for c in over[p]:
            c.wait_recv()
    for c in started:
        c.wait_send()


def pair_kernel(
    all0, all1, all2, hq, hr, fw, fl, centre_ref,
    out0, out1, out2,
    comp, sums, factor, raw, counts, count, sem,
):
    outs = (out0, out1, out2)
    marked = jnp.where(all0[...] < 1e29, 0.5, 0.0)
    marked = jnp.sum(marked, axis=1).astype(bf16)
    counted = lax.dot_general(
        jnp.ones((8, 128), bf16), marked, (((1,), (1,)), ((), ())), preferred_element_type=f32
    )
    counts[...] = counted.astype(jnp.int32)
    copy = pltpu.make_async_copy(counts, count, sem)
    copy.start()
    copy.wait()

    lane = lax.broadcasted_iota(jnp.int32, (8, 128), 1)
    blank = jnp.zeros((2, SLOTS), f32)

    def pack(o, offset):
        shift = offset % 128
        base = pl.multiple_of(offset - shift, 128)
        x = jnp.concatenate([unfold((all0[o], all1[o], all2[o])), blank], axis=0)
        x = jnp.concatenate([x, jnp.zeros((8, 128), f32)], axis=1)
        x = pltpu.roll(x, shift, 1)
        first = pl.ds(base, 128)
        comp[:, first] = jnp.where(lane < shift, comp[:, first], x[:, 0:128])
        comp[:, pl.ds(base + 128, SLOTS)] = x[:, 128:]
        return offset + count[0, o]

    total = lax.fori_loop(0, OWNERS, pack, jnp.int32(0))
    blocks = (total + BLOCK - 1) // BLOCK
    centre = centre_ref[:, 0:1]
    row = lax.broadcasted_iota(jnp.int32, (8, 1), 0)
    scale = jnp.where(row < 3, POS_SCALE, VEL_SCALE)

    def columns(i):
        return pl.ds(pl.multiple_of(i * BLOCK, BLOCK), BLOCK)

    def make_factor(i):
        t = (comp[:, columns(i)] - centre) * scale
        square = t[0:1] * t[0:1] + t[1:2] * t[1:2] + t[2:3] * t[2:3] + soften * POS_SCALE**2
        product = t[0:1] * t[3:4] + t[1:2] * t[4:5] + t[2:3] * t[5:6]
        a, b, c = split3(jnp.concatenate([t[0:6], square, product], axis=0))
        ones = jnp.ones((8, BLOCK), f32)
        fill = jnp.zeros((72, BLOCK), f32)
        factor[...] = jnp.concatenate([a, a, b, b, a, c, ones, fill], axis=0).astype(bf16)

    def combine(i):
        sw = raw[0:8] + (raw[8:16] + raw[16:24]) + (raw[64:72] + raw[72:80])
        sb = raw[32:40] + (raw[40:48] + raw[48:56]) + (raw[80:88] + raw[88:96])
        t = comp[:, columns(i)] - centre
        rw = (sw - t * sw[6:7]) * (1.0 / W_SCALE)
        rb = pltpu.roll(sb - t * sb[6:7], 3, 0)
        sums[:, columns(i)] = rw - jnp.where((row >= 3) & (row < 6), 3.0 * rb, 0.0)

    def block(i, carry):
        combine(jnp.maximum(i - 1, 0))
        g = factor[...]
        sw = jnp.zeros((32, BLOCK), f32)
        sb = jnp.zeros((32, BLOCK), f32)
        lw = jnp.zeros((32, BLOCK), f32)
        lb = jnp.zeros((32, BLOCK), f32)
        for first in range(0, STARS, CHUNK):
            part = slice(first, first + CHUNK)
            q = jnp.dot(hq[part], g, preferred_element_type=f32)
            rv = jnp.dot(hr[part], g, preferred_element_type=f32)
            inv = lax.rsqrt(q)
            inv2 = inv * inv
            w = inv2 * inv
            b = w * inv2 * rv
            w_high = w.astype(bf16)
            b_high = b.astype(bf16)
            w_low = (w - w_high.astype(f32)).astype(f8)
            b_low = (b - b_high.astype(f32)).astype(f8)
            sw += jnp.dot(fw[:, part], w_high, preferred_element_type=f32)
            sb += jnp.dot(fw[:, part], b_high, preferred_element_type=f32)
            lw += jnp.dot(fl[:, part], w_low, preferred_element_type=f32)
            lb += jnp.dot(fl[:, part], b_low, preferred_element_type=f32)
        raw[0:32] = sw
        raw[32:64] = sb
        raw[64:80] = lw[0:16]
        raw[80:96] = lb[0:16]
        make_factor(i + 1)
        return carry

    raw[...] = jnp.zeros_like(raw)
    make_factor(0)
    lax.fori_loop(0, blocks, block, 0)
    combine(jnp.maximum(blocks - 1, 0))

    def unpack(o, offset):
        shift = offset % 128
        base = pl.multiple_of(offset - shift, 128)
        x = sums[:, pl.ds(base, SLOTS + 128)]
        x = pltpu.roll(x, (SLOTS + 128) - shift, 1)
        for p in range(PAIRS):
            outs[p][o] = fold(x[2 * p:2 * p + 2, 0:SLOTS])
        return offset + count[0, o]

    lax.fori_loop(0, OWNERS, unpack, jnp.int32(0))


def reduce_kernel(
    part0, part1, part2, start_ref, count_ref, out_ref,
    got_core, got_1, got_2, got_3, sum_1, sum_2, send_sem, recv_sem,
):
    part = (part0, part1, part2)
    barrier = greet()
    me, core = place()
    started = []

    def send(p, phase, k, src, dst, target):
        c = pltpu.make_async_remote_copy(
            src_ref=src, dst_ref=dst, send_sem=send_sem.at[p, phase, k],
            recv_sem=recv_sem.at[p, phase, k], device_id=target, device_id_type=MESH,
        )
        c.start()
        started.append(c)
        return c

    def plane(p, d):
        axis = REDUCE_ORDER[p][0][0]
        return {"x": None, "y": None, "z": None, axis: (me[axis] + d) % 4}

    pl.semaphore_wait(barrier, 10)
    over = [[None] * PAIRS for _ in range(5)]
    for d in (1, 2, 3, 4):
        for p in range(PAIRS):
            over[d][p] = send(
                p, 0, d - 1, view(part[p], plane(p, d), 1 - core), got_core[p].at[d - 1],
                device(me, 1 - core),
            )
    first = [[] for _ in range(PAIRS)]
    for d in (1, 2, 3, 4):
        for p in range(PAIRS):
            over[d][p].wait_recv()
            sum_1[p][d - 1] = view(part[p], plane(p, d), core)[...] + got_core[p][d - 1]
            if d < 4:
                axis = REDUCE_ORDER[p][0][0]
                first[p].append(send(
                    p, 1, d - 1, sum_1[p].at[d - 1], got_1[p].at[d - 1],
                    along(me, core, axis, d),
                ))
    second = [[] for _ in range(PAIRS)]
    for p in range(PAIRS):
        axes, _, _, at2, _ = REDUCE_ORDER[p]
        for c in first[p]:
            c.wait_recv()
        sum_1[p][3] = sum_1[p][3] + (got_1[p][0] + got_1[p][1] + got_1[p][2])
        for d in (1, 2, 3):
            second[p].append(send(
                p, 2, d - 1, at2(sum_1[p].at[3], (me[axes[1]] + d) % 4), got_2[p].at[d - 1],
                along(me, core, axes[1], d),
            ))
    third = [[] for _ in range(PAIRS)]
    for p in range(PAIRS):
        axes, _, _, at2, at3 = REDUCE_ORDER[p]
        for c in second[p]:
            c.wait_recv()
        own = at2(sum_1[p].at[3], me[axes[1]])[...]
        sum_2[p][...] = own + (got_2[p][0] + got_2[p][1] + got_2[p][2])
        for d in (1, 2, 3):
            third[p].append(send(
                p, 3, d - 1, at3(sum_2[p], (me[axes[2]] + d) % 4), got_3[p].at[d - 1],
                along(me, core, axes[2], d),
            ))
    blocks = []
    for p in range(PAIRS):
        axes, _, _, _, at3 = REDUCE_ORDER[p]
        for c in third[p]:
            c.wait_recv()
        own = at3(sum_2[p], me[axes[2]])[...]
        blocks.append(own + (got_3[p][0] + got_3[p][1] + got_3[p][2]))

    total = unfold(blocks) * (1.0 / (STARS * OWNERS))
    start = start_ref[...]
    step = start[12:13]
    acc0, jerk0 = start[6:9], start[9:12]
    acc1, jerk1 = total[0:3], total[3:6]
    vel1 = start[3:6] + (acc0 + acc1) * step / 2.0 + (jerk0 - jerk1) * step * step / 12.0
    pos1 = start[0:3] + (start[3:6] + vel1) * step / 2.0 + (acc0 - acc1) * step * step / 12.0
    state = jnp.concatenate([pos1, vel1, acc1, jerk1], axis=0)
    live = lax.broadcasted_iota(jnp.int32, (12, SLOTS), 1) < count_ref[0]
    out_ref[...] = jnp.where(live, state, 0.0)
    for c in started:
        c.wait_send()


def shards(
    positions, velocities, old_acc, old_jerk, masses, elapsed, levels, active_index, active_count
):
    def lines(a):
        return a.reshape(STARS // 128, 128)

    def params(collective_id=None):
        extra = {} if collective_id is None else {
            "collective_id": collective_id, "has_side_effects": True
        }
        return pltpu.CompilerParams(vmem_limit_bytes=VMEM_LIMIT, **extra)

    *every, start, hq, hr, fw, fl, centre = pl.pallas_call(
        gather_kernel,
        out_shape=[jax.ShapeDtypeStruct(PLACES, f32)] * PAIRS + [
            jax.ShapeDtypeStruct((16, SLOTS), f32),
            jax.ShapeDtypeStruct((STARS, 128), bf16),
            jax.ShapeDtypeStruct((STARS, 128), bf16),
            jax.ShapeDtypeStruct((32, STARS), bf16),
            jax.ShapeDtypeStruct((32, STARS), f8),
            jax.ShapeDtypeStruct((8, 128), f32),
        ],
        in_specs=[vmem()] * 8 + [smem()],
        out_specs=[vmem()] * (PAIRS + 6),
        scratch_shapes=[
            pltpu.VMEM((16, STARS), f32),
            pltpu.SemaphoreType.DMA((PAIRS, 4, 4)),
            pltpu.SemaphoreType.DMA((PAIRS, 4, 4)),
        ],
        compiler_params=params(0),
        name="predict_gather",
    )(
        positions, velocities, old_acc, old_jerk, lines(masses), lines(elapsed), lines(levels),
        active_index, active_count,
    )
    parts = pl.pallas_call(
        pair_kernel,
        out_shape=[jax.ShapeDtypeStruct((OWNERS, 8, 128), f32)] * PAIRS,
        in_specs=[vmem()] * 8,
        out_specs=[vmem()] * PAIRS,
        scratch_shapes=[
            pltpu.VMEM((8, ROOM), f32),
            pltpu.VMEM((8, ROOM), f32),
            pltpu.VMEM((128, BLOCK), bf16),
            pltpu.VMEM((96, BLOCK), f32),
            pltpu.VMEM((8, 128), jnp.int32),
            pltpu.SMEM((8, 128), jnp.int32),
            pltpu.SemaphoreType.DMA,
        ],
        compiler_params=params(),
        name="pair_sums",
    )(*[e.reshape(OWNERS, 8, 128) for e in every], hq, hr, fw, fl, centre)

    def buffers(count, which):
        head = () if count is None else (count,)
        return [pltpu.VMEM(head + order[which] + (8, 128), f32) for order in REDUCE_ORDER]

    return pl.pallas_call(
        reduce_kernel,
        out_shape=jax.ShapeDtypeStruct((12, SLOTS), f32),
        in_specs=[vmem()] * (PAIRS + 1) + [smem()],
        out_specs=vmem(),
        scratch_shapes=[
            buffers(4, 1),
            buffers(3, 1),
            buffers(3, 2),
            [pltpu.VMEM((3, 8, 128), f32)] * PAIRS,
            buffers(4, 1),
            buffers(None, 2),
            pltpu.SemaphoreType.DMA((PAIRS, 4, 4)),
            pltpu.SemaphoreType.DMA((PAIRS, 4, 4)),
        ],
        compiler_params=params(1),
        name="reduce_correct",
    )(*[p.reshape(PLACES) for p in parts], start, active_count)


def solution(mesh):
    every = ("ia", "ja")
    in_specs = (
        P(None, every), P(None, every), P(None, every), P(None, every),
        P(every), P(every), P(every), P(every, None), P(every),
    )
    return jax.shard_map(
        shards, mesh=mesh, in_specs=in_specs, out_specs=P(None, every), check_vma=False
    )
```

time: 218 us -> 202 us (0.927)
  Pallas kernels: 207 us -> 199 us
  other arithmetic: 3.91 us -> 0 us
  local copies, waits for them, and re-layouts: 5.26 us -> 1.38 us
    pallas_call x1, Pallas kernels: 27 us -> 16.9 us  [shards(): pl.pallas_call(reduce_kernel, out_shape=jax.ShapeDtypeStruct((12, SLOTS),...]
    convert_element_type x1 -> x0, other arithmetic: 3.91 us -> none  [shards(): counts = every[:, 6, 0].astype(jnp.int32)]
    reshape x3 -> x0, local copies, waits for them, and re-layouts: 3.88 us -> none  [the longest x1 1.3 us: shards(): elapsed.reshape(1, STARS)]
where the time goes in v2:
time: 202 us; the launch traced here: 201 us
  Pallas kernels  199 us (99%)
    pallas_call x1, Pallas kernels, shards(): pl.pallas_call(pair_kernel, out_shape=[jax.ShapeDtypeStruct((OWNERS, 8, 1...  157 us
    pallas_call x1, Pallas kernels, shards(): pl.pallas_call(gather_kernel, out_shape=[jax.ShapeDtypeStruct(PLACES, f32...  24.4 us
    pallas_call x1, Pallas kernels, shards(): pl.pallas_call(reduce_kernel, out_shape=jax.ShapeDtypeStruct((12, SLOTS),...  16.9 us

profile of v2, /device:TPU:1, one launch (start us, length us, event | category | flops | bytes accessed | tf_op | source)
XLA Modules:
  0.0 200.7 jit_solution(2494175957326068423)
XLA Ops:
  0.7 24.4 %predict_gather.1 = (f32[4,2,4,2,2,8,128]{6,5,4,3,2,1,0:T(8,128)}, f32[4,2,4,2,2,8,128]{6,5,4,3,2,1,0:T(8,128)}, f32[4,2,4,2,2,8,128]{6,5,4,3,2,1,0:T(8,128)}, f...) custom-call(f32[3,1536]{1,0:T(4,128)} %pos_ref.1, ...), custom_call_target="tpu_custom_call" | custom-call | tf_op jit(solution)/shard_map/predict_gather/pallas_call | solution.py:417
  25.0 157.4 %pair_sums.1 = (f32[128,8,128]{2,1,0:T(8,128)}, f32[128,8,128]{2,1,0:T(8,128)}, f32[128,8,128]{2,1,0:T(8,128)}) custom-call(f32[128,8,128]{2,1,0:T(8,128)} %bitcast.9, f32[128,8,128]{2,1,0:T(8,128)} %bitcast.10, f32[128,8,128]{2,1,0:T(8,128)} %bitcast.11, bf16[1536,128]{1,0:T(8,128)(2,1)} %get-tuple-element.20.hq, bf16[1536,128]{1,0:T(8,128)(2,1)} %get-tuple-element.21.hr, ...), custom_call_target="tpu_custom_call" | custom-call | tf_op jit(solution)/shard_map/pair_sums/pallas_call | solution.py:440
  182.4 16.9 %reduce_correct.1 = f32[12,512]{1,0:T(8,128)} custom-call(f32[4,2,4,2,2,8,128]{6,5,4,3,2,1,0:T(8,128)} %bitcast.12, f32[4,2,4,2,2,8,128]{6,5,4,3,2,1,0:T(8,128)} %bitcast.13, f32[4,2,4,2,2,8,128]{6,5,4,3,2,1,0:T(8,128)} %bitcast.14, f32[16,512]{1,0:T(8,128)} %get-tuple-element.28.start_ref, s32[1]{0:T(128)S(6)} %copy.11.count_ref), custom_call_target="tpu_custom_call" | custom-call | tf_op jit(solution)/shard_map/reduce_correct/pallas_call | solution.py:462
  199.3 1.4 copy.12

commit v3 on v2

--- a/solution.py
+++ b/solution.py
@@ -243,7 +243,7 @@
         comp[:, pl.ds(base + 128, SLOTS)] = x[:, 128:]
         return offset + count[0, o]
 
-    total = lax.fori_loop(0, OWNERS, pack, jnp.int32(0))
+    total = lax.fori_loop(0, OWNERS, pack, jnp.int32(0), unroll=16)
     blocks = (total + BLOCK - 1) // BLOCK
     centre = centre_ref[:, 0:1]
     row = lax.broadcasted_iota(jnp.int32, (8, 1), 0)
@@ -313,7 +313,7 @@
             outs[p][o] = fold(x[2 * p:2 * p + 2, 0:SLOTS])
         return offset + count[0, o]
 
-    lax.fori_loop(0, OWNERS, unpack, jnp.int32(0))
+    lax.fori_loop(0, OWNERS, unpack, jnp.int32(0), unroll=16)
 
 
 def reduce_kernel(

time: 202 us -> 186 us (0.921)
  Pallas kernels: 199 us -> 183 us
    pallas_call x1, Pallas kernels: 157 us -> 142 us  [shards(): pl.pallas_call(pair_kernel, out_shape=[jax.ShapeDtypeStruct((OWNERS, 8, 1...]
where the time goes in v3:
time: 186 us; the launch traced here: 185 us
  Pallas kernels  183 us (98%)
    pallas_call x1, Pallas kernels, shards(): pl.pallas_call(pair_kernel, out_shape=[jax.ShapeDtypeStruct((OWNERS, 8, 1...  142 us
    pallas_call x1, Pallas kernels, shards(): pl.pallas_call(gather_kernel, out_shape=[jax.ShapeDtypeStruct(PLACES, f32...  24.4 us
    pallas_call x1, Pallas kernels, shards(): pl.pallas_call(reduce_kernel, out_shape=jax.ShapeDtypeStruct((12, SLOTS),...  16.9 us

profile of v3, /device:TPU:1, one launch (start us, length us, event | category | flops | bytes accessed | tf_op | source)
XLA Modules:
  0.0 185.2 jit_solution(16593964988326135205)
XLA Ops:
  0.7 24.4 %predict_gather.1 = (f32[4,2,4,2,2,8,128]{6,5,4,3,2,1,0:T(8,128)}, f32[4,2,4,2,2,8,128]{6,5,4,3,2,1,0:T(8,128)}, f32[4,2,4,2,2,8,128]{6,5,4,3,2,1,0:T(8,128)}, f...) custom-call(f32[3,1536]{1,0:T(4,128)} %pos_ref.1, ...), custom_call_target="tpu_custom_call" | custom-call | tf_op jit(solution)/shard_map/predict_gather/pallas_call | solution.py:417
  25.0 141.9 %pair_sums.1 = (f32[128,8,128]{2,1,0:T(8,128)}, f32[128,8,128]{2,1,0:T(8,128)}, f32[128,8,128]{2,1,0:T(8,128)}) custom-call(f32[128,8,128]{2,1,0:T(8,128)} %bitcast.9, f32[128,8,128]{2,1,0:T(8,128)} %bitcast.10, f32[128,8,128]{2,1,0:T(8,128)} %bitcast.11, bf16[1536,128]{1,0:T(8,128)(2,1)} %get-tuple-element.20.hq, bf16[1536,128]{1,0:T(8,128)(2,1)} %get-tuple-element.21.hr, ...), custom_call_target="tpu_custom_call" | custom-call | tf_op jit(solution)/shard_map/pair_sums/pallas_call | solution.py:440
  166.9 16.9 %reduce_correct.1 = f32[12,512]{1,0:T(8,128)} custom-call(f32[4,2,4,2,2,8,128]{6,5,4,3,2,1,0:T(8,128)} %bitcast.12, f32[4,2,4,2,2,8,128]{6,5,4,3,2,1,0:T(8,128)} %bitcast.13, f32[4,2,4,2,2,8,128]{6,5,4,3,2,1,0:T(8,128)} %bitcast.14, f32[16,512]{1,0:T(8,128)} %get-tuple-element.28.start_ref, s32[1]{0:T(128)S(6)} %copy.11.count_ref), custom_call_target="tpu_custom_call" | custom-call | tf_op jit(solution)/shard_map/reduce_correct/pallas_call | solution.py:462
  183.8 1.4 copy.12

commit v4 on v3

--- a/solution.py
+++ b/solution.py
@@ -15,7 +15,7 @@
 SLOTS = 512
 OWNERS = 128
 BLOCK = 256
-CHUNK = 768
+CHUNK = 256
 ROOM = OWNERS * SLOTS + SLOTS + 128
 VMEM_LIMIT = 56 * 2**20
 PAIRS = 3
@@ -196,7 +196,7 @@
     product = pos[0:1] * vel[0:1] + pos[1:2] * vel[1:2] + pos[2:3] * vel[2:3]
     hr_ref[...] = factors(jnp.concatenate([-vel, -pos], axis=0), product, 7)
     fill = jnp.zeros((8, STARS), f32)
-    fw_ref[...] = jnp.concatenate(split3(weights) + (fill,), axis=0).astype(bf16)
+    fw_ref[...] = jnp.concatenate(split3(weights)[0:2], axis=0).astype(bf16)
     high = weights.astype(f8).astype(f32)
     f8_ref[...] = jnp.concatenate([high, weights - high, fill, fill], axis=0).astype(f8)
 
@@ -220,10 +220,8 @@
 ):
     outs = (out0, out1, out2)
     marked = jnp.where(all0[...] < 1e29, 0.5, 0.0)
-    marked = jnp.sum(marked, axis=1).astype(bf16)
-    counted = lax.dot_general(
-        jnp.ones((8, 128), bf16), marked, (((1,), (1,)), ((), ())), preferred_element_type=f32
-    )
+    counted = jnp.sum(jnp.sum(marked, axis=1), axis=1, keepdims=True)
+    counted = jnp.broadcast_to(counted, (OWNERS, 128)).T[0:8]
     counts[...] = counted.astype(jnp.int32)
     copy = pltpu.make_async_copy(counts, count, sem)
     copy.start()
@@ -258,51 +256,89 @@
         product = t[0:1] * t[3:4] + t[1:2] * t[4:5] + t[2:3] * t[5:6]
         a, b, c = split3(jnp.concatenate([t[0:6], square, product], axis=0))
         ones = jnp.ones((8, BLOCK), f32)
-        fill = jnp.zeros((72, BLOCK), f32)
+        fill = jnp.zeros((200, BLOCK), f32)
         factor[...] = jnp.concatenate([a, a, b, b, a, c, ones, fill], axis=0).astype(bf16)
 
     def combine(i):
-        sw = raw[0:8] + (raw[8:16] + raw[16:24]) + (raw[64:72] + raw[72:80])
-        sb = raw[32:40] + (raw[40:48] + raw[48:56]) + (raw[80:88] + raw[88:96])
+        sw = raw[0:8] + (raw[8:16] + (raw[32:40] + raw[40:48]))
+        sb = raw[16:24] + (raw[24:32] + (raw[64:72] + raw[72:80]))
         t = comp[:, columns(i)] - centre
         rw = (sw - t * sw[6:7]) * (1.0 / W_SCALE)
         rb = pltpu.roll(sb - t * sb[6:7], 3, 0)
         sums[:, columns(i)] = rw - jnp.where((row >= 3) & (row < 6), 3.0 * rb, 0.0)
 
-    def block(i, carry):
-        combine(jnp.maximum(i - 1, 0))
-        g = factor[...]
-        sw = jnp.zeros((32, BLOCK), f32)
-        sb = jnp.zeros((32, BLOCK), f32)
-        lw = jnp.zeros((32, BLOCK), f32)
-        lb = jnp.zeros((32, BLOCK), f32)
-        for first in range(0, STARS, CHUNK):
-            part = slice(first, first + CHUNK)
-            q = jnp.dot(hq[part], g, preferred_element_type=f32)
-            rv = jnp.dot(hr[part], g, preferred_element_type=f32)
-            inv = lax.rsqrt(q)
-            inv2 = inv * inv
-            w = inv2 * inv
-            b = w * inv2 * rv
-            w_high = w.astype(bf16)
-            b_high = b.astype(bf16)
-            w_low = (w - w_high.astype(f32)).astype(f8)
-            b_low = (b - b_high.astype(f32)).astype(f8)
-            sw += jnp.dot(fw[:, part], w_high, preferred_element_type=f32)
-            sb += jnp.dot(fw[:, part], b_high, preferred_element_type=f32)
-            lw += jnp.dot(fl[:, part], w_low, preferred_element_type=f32)
-            lb += jnp.dot(fl[:, part], b_low, preferred_element_type=f32)
-        raw[0:32] = sw
-        raw[32:64] = sb
-        raw[64:80] = lw[0:16]
-        raw[80:96] = lb[0:16]
-        make_factor(i + 1)
-        return carry
-
-    raw[...] = jnp.zeros_like(raw)
-    make_factor(0)
-    lax.fori_loop(0, blocks, block, 0)
-    combine(jnp.maximum(blocks - 1, 0))
+    def products(acc_q, acc_r, acc_w, acc_b, acc_lw, acc_lb):
+        def stage_one(c, buffer, load):
+            part = slice(c * CHUNK, (c + 1) * CHUNK)
+            blank = jnp.zeros((CHUNK, 128), bf16)
+            pltpu.matmul_acc_lhs(
+                acc_q[buffer], jnp.concatenate([hq[part], blank], axis=1), load_staged_rhs=load
+            )
+            pltpu.matmul_acc_lhs(acc_r[buffer], jnp.concatenate([hr[part], blank], axis=1))
+
+        def stage_factor(i):
+            make_factor(i)
+            pltpu.matmul_push_rhs(factor[...], 0, 0)
+
+        def pop_sums():
+            raw[0:16] = pltpu.matmul_pop(acc_w)
+            raw[16:32] = pltpu.matmul_pop(acc_b)
+            raw[32:64] = pltpu.matmul_pop(acc_lw)
+            raw[64:96] = pltpu.matmul_pop(acc_lb)
+
+        chunks = STARS // CHUNK
+
+        def block(i, carry):
+            for c in range(chunks):
+                if c == chunks - 1:
+                    stage_factor(i + 1)
+                    stage_one(0, 0, 0)
+                else:
+                    stage_one(c + 1, (c + 1) % 2, None)
+                q = pltpu.matmul_pop(acc_q[c % 2])
+                rv = pltpu.matmul_pop(acc_r[c % 2])
+                inv = lax.rsqrt(q)
+                inv2 = inv * inv
+                w = inv2 * inv
+                b = w * inv2 * rv
+                w_high = w.astype(bf16)
+                b_high = b.astype(bf16)
+                w_low = (w - w_high.astype(f32)).astype(f8)
+                b_low = (b - b_high.astype(f32)).astype(f8)
+                if c == 0:
+                    pop_sums()
+                part = slice(c * CHUNK, (c + 1) * CHUNK)
+                pltpu.matmul_push_rhs(w_high, 0, 1)
+                pltpu.matmul_acc_lhs(acc_w, fw[:, part], load_staged_rhs=0)
+                pltpu.matmul_push_rhs(b_high, 1, 1)
+                pltpu.matmul_acc_lhs(acc_b, fw[:, part], load_staged_rhs=1)
+                pltpu.matmul_push_rhs(w_low, 0, 1)
+                pltpu.matmul_acc_lhs(acc_lw, fl[:, part], load_staged_rhs=0)
+                pltpu.matmul_push_rhs(b_low, 1, 1)
+                pltpu.matmul_acc_lhs(acc_lb, fl[:, part], load_staged_rhs=1)
+                if c == 0:
+                    combine(jnp.maximum(i - 1, 0))
+            return carry
+
+        pop_sums()
+        for k in range(2):
+            pltpu.matmul_pop(acc_q[k])
+            pltpu.matmul_pop(acc_r[k])
+        stage_factor(0)
+        stage_one(0, 0, 0)
+        lax.fori_loop(0, blocks, block, 0)
+        pltpu.matmul_pop(acc_q[0])
+        pltpu.matmul_pop(acc_r[0])
+        pop_sums()
+        combine(jnp.maximum(blocks - 1, 0))
+
+    pl.run_scoped(
+        products,
+        [pltpu.ACC(0)((CHUNK, BLOCK), f32)] * 2,
+        [pltpu.ACC(0)((CHUNK, BLOCK), f32)] * 2,
+        *[pltpu.ACC(1)((16, BLOCK), f32)] * 2,
+        *[pltpu.ACC(1)((32, BLOCK), f32)] * 2,
+    )
 
     def unpack(o, offset):
         shift = offset % 128
@@ -314,6 +350,18 @@
         return offset + count[0, o]
 
     lax.fori_loop(0, OWNERS, unpack, jnp.int32(0), unroll=16)
+
+
+def pair_scratch():
+    return [
+        pltpu.VMEM((8, ROOM), f32),
+        pltpu.VMEM((8, ROOM), f32),
+        pltpu.VMEM((256, BLOCK), bf16),
+        pltpu.VMEM((96, BLOCK), f32),
+        pltpu.VMEM((8, 128), jnp.int32),
+        pltpu.SMEM((8, 128), jnp.int32),
+        pltpu.SemaphoreType.DMA,
+    ]
 
 
 def reduce_kernel(
@@ -420,7 +468,7 @@
             jax.ShapeDtypeStruct((16, SLOTS), f32),
             jax.ShapeDtypeStruct((STARS, 128), bf16),
             jax.ShapeDtypeStruct((STARS, 128), bf16),
-            jax.ShapeDtypeStruct((32, STARS), bf16),
+            jax.ShapeDtypeStruct((16, STARS), bf16),
             jax.ShapeDtypeStruct((32, STARS), f8),
             jax.ShapeDtypeStruct((8, 128), f32),
         ],
@@ -442,15 +490,7 @@
         out_shape=[jax.ShapeDtypeStruct((OWNERS, 8, 128), f32)] * PAIRS,
         in_specs=[vmem()] * 8,
         out_specs=[vmem()] * PAIRS,
-        scratch_shapes=[
-            pltpu.VMEM((8, ROOM), f32),
-            pltpu.VMEM((8, ROOM), f32),
-            pltpu.VMEM((128, BLOCK), bf16),
-            pltpu.VMEM((96, BLOCK), f32),
-            pltpu.VMEM((8, 128), jnp.int32),
-            pltpu.SMEM((8, 128), jnp.int32),
-            pltpu.SemaphoreType.DMA,
-        ],
+        scratch_shapes=pair_scratch(),
         compiler_params=params(),
         name="pair_sums",
     )(*[e.reshape(OWNERS, 8, 128) for e in every], hq, hr, fw, fl, centre)

time: 186 us -> 165 us (0.89)
  Pallas kernels: 183 us -> 162 us
    pallas_call x1, Pallas kernels: 142 us -> 121 us  [shards(): pl.pallas_call(pair_kernel, out_shape=[jax.ShapeDtypeStruct((OWNERS, 8, 1...]
where the time goes in v4:
time: 165 us; the launch traced here: 164 us
  Pallas kernels  162 us (98%)
    pallas_call x1, Pallas kernels, shards(): pl.pallas_call(pair_kernel, out_shape=[jax.ShapeDtypeStruct((OWNERS, 8, 1...  121 us
    pallas_call x1, Pallas kernels, shards(): pl.pallas_call(gather_kernel, out_shape=[jax.ShapeDtypeStruct(PLACES, f32...  24.4 us
    pallas_call x1, Pallas kernels, shards(): pl.pallas_call(reduce_kernel, out_shape=jax.ShapeDtypeStruct((12, SLOTS),...  17 us

profile of v4, /device:TPU:1, one launch (start us, length us, event | category | flops | bytes accessed | tf_op | source)
XLA Modules:
  0.0 164.1 jit_solution(1624880762647398824)
XLA Ops:
  0.7 24.4 %predict_gather.1 = (f32[4,2,4,2,2,8,128]{6,5,4,3,2,1,0:T(8,128)}, f32[4,2,4,2,2,8,128]{6,5,4,3,2,1,0:T(8,128)}, f32[4,2,4,2,2,8,128]{6,5,4,3,2,1,0:T(8,128)}, f...) custom-call(f32[3,1536]{1,0:T(4,128)} %pos_ref.1, ...), custom_call_target="tpu_custom_call" | custom-call | tf_op jit(solution)/shard_map/predict_gather/pallas_call | solution.py:465
  25.0 120.7 %pair_sums.1 = (f32[128,8,128]{2,1,0:T(8,128)}, f32[128,8,128]{2,1,0:T(8,128)}, f32[128,8,128]{2,1,0:T(8,128)}) custom-call(f32[128,8,128]{2,1,0:T(8,128)} %bitcast.9, f32[128,8,128]{2,1,0:T(8,128)} %bitcast.10, f32[128,8,128]{2,1,0:T(8,128)} %bitcast.11, bf16[1536,128]{1,0:T(8,128)(2,1)} %get-tuple-element.20.hq, bf16[1536,128]{1,0:T(8,128)(2,1)} %get-tuple-element.21.hr, ...), custom_call_target="tpu_custom_call" | custom-call | tf_op jit(solution)/shard_map/pair_sums/pallas_call | solution.py:488
  145.7 17.0 %reduce_correct.1 = f32[12,512]{1,0:T(8,128)} custom-call(f32[4,2,4,2,2,8,128]{6,5,4,3,2,1,0:T(8,128)} %bitcast.12, f32[4,2,4,2,2,8,128]{6,5,4,3,2,1,0:T(8,128)} %bitcast.13, f32[4,2,4,2,2,8,128]{6,5,4,3,2,1,0:T(8,128)} %bitcast.14, f32[16,512]{1,0:T(8,128)} %get-tuple-element.28.start_ref, s32[1]{0:T(128)S(6)} %copy.11.count_ref), custom_call_target="tpu_custom_call" | custom-call | tf_op jit(solution)/shard_map/reduce_correct/pallas_call | solution.py:502
  162.7 1.4 copy.12

commit v5 on v4

--- a/solution.py
+++ b/solution.py
@@ -17,15 +17,10 @@
 BLOCK = 256
 CHUNK = 256
 ROOM = OWNERS * SLOTS + SLOTS + 128
-VMEM_LIMIT = 56 * 2**20
+VMEM_LIMIT = 24 * 2**20
 PAIRS = 3
-GATHER_ORDER = ("xyz", "yzx", "zxy")
-REDUCE_ORDER = (
-    ("zyx", (2, 4, 2), (2, 2), lambda r, j: r.at[:, j], lambda r, j: r.at[j // 2, j % 2]),
-    ("xzy", (4, 4), (4,), lambda r, j: r.at[j], lambda r, j: r.at[j]),
-    ("yxz", (4, 2, 2), (4,), lambda r, j: r.at[:, j // 2, j % 2], lambda r, j: r.at[j]),
-)
-PLACES = (4, 2, 4, 2, 2, 8, 128)
+AXES = ("xyz", "yzx", "zxy")
+PLACES = (2, 4, 16, 8, 128)
 POS_SCALE = 2.0**-2
 VEL_SCALE = 2.0**-8
 W_SCALE = 2.0**6
@@ -57,13 +52,6 @@
 
 def along(me, core, axis, d):
     return device({**me, axis: (me[axis] + d) % 4}, core)
-
-
-def view(ref, at, core):
-    xh, xl = (slice(None),) * 2 if at["x"] is None else (at["x"] // 2, at["x"] % 2)
-    z = slice(None) if at["z"] is None else at["z"]
-    y = slice(None) if at["y"] is None else at["y"]
-    return ref.at[z, xh, y, xl, core]
 
 
 def greet():
@@ -135,28 +123,32 @@
     start_ref[...] = start
     target = jnp.concatenate(predict(start, start[12:13]), axis=0)
     live = lax.broadcasted_iota(jnp.int32, (8, SLOTS), 1) < count_ref[0]
-    view(all0, me, core)[...] = fold(jnp.where(live[0:2], target[0:2], 1e30))
-    view(all1, me, core)[...] = fold(target[2:4])
-    view(all2, me, core)[...] = fold(target[4:6])
+    pairs = (jnp.where(live[0:2], target[0:2], 1e30), target[2:4], target[4:6])
+    for p in range(PAIRS):
+        one, two, three = (me[axis] for axis in AXES[p])
+        every[p][core, three, one * 4 + two] = fold(pairs[p])
 
     pl.semaphore_wait(barrier, 10)
 
-    have = [dict(me) for _ in range(PAIRS)]
     flight = [[] for _ in range(PAIRS)]
 
     def begin(phase):
         for p in range(PAIRS):
-            axis = GATHER_ORDER[p][phase]
+            one, two, three = (me[axis] for axis in AXES[p])
+            block = every[p].at[core, three]
+            if phase == 0:
+                block = block.at[one * 4 + two]
+            elif phase == 1:
+                block = block.at[pl.ds(one * 4, 4)]
+            axis = AXES[p][(1, 0, 2)[phase]]
             flight[p] = [
-                send(p, phase, d - 1, view(every[p], have[p], core), along(me, core, axis, d))
-                for d in (1, 2, 3)
+                send(p, phase, d - 1, block, along(me, core, axis, d)) for d in (1, 2, 3)
             ]
 
-    def finish(phase):
+    def finish():
         for p in range(PAIRS):
             for c in flight[p]:
                 c.wait_recv()
-            have[p][GATHER_ORDER[p][phase]] = None
 
     begin(0)
     chosen = lax.dot_general(
@@ -165,7 +157,7 @@
     )[0:1]
     interval = jnp.where(chosen > 0.5, step, flat(elapsed_ref))
     src = jnp.concatenate(predict(state[...], interval), axis=0)
-    finish(0)
+    finish()
     begin(1)
 
     centre = jnp.sum(src, axis=1, keepdims=True) * (1.0 / STARS)
@@ -187,10 +179,10 @@
 
     square = pos[0:1] * pos[0:1] + pos[1:2] * pos[1:2] + pos[2:3] * pos[2:3]
     hq_ref[...] = factors(jnp.concatenate([pos * -2.0, zero, zero, zero], axis=0), square, 6)
-    finish(1)
+    finish()
     begin(2)
     over = [
-        [send(p, 3, 0, view(every[p], have[p], core), device(me, 1 - core))]
+        [send(p, 3, 0, every[p].at[core, me[AXES[p][2]]], device(me, 1 - core))]
         for p in range(PAIRS)
     ]
     product = pos[0:1] * vel[0:1] + pos[1:2] * vel[1:2] + pos[2:3] * vel[2:3]
@@ -202,10 +194,9 @@
 
     for d in (1, 2, 3):
         for p in range(PAIRS):
-            axis = GATHER_ORDER[p][2]
             flight[p][d - 1].wait_recv()
-            came = {**have[p], axis: (me[axis] - d + 4) % 4}
-            over[p].append(send(p, 3, d, view(every[p], came, core), device(me, 1 - core)))
+            came = (me[AXES[p][2]] - d + 4) % 4
+            over[p].append(send(p, 3, d, every[p].at[core, came], device(me, 1 - core)))
     for p in range(PAIRS):
         for c in over[p]:
             c.wait_recv()
@@ -230,18 +221,34 @@
     lane = lax.broadcasted_iota(jnp.int32, (8, 128), 1)
     blank = jnp.zeros((2, SLOTS), f32)
 
-    def pack(o, offset):
+    def owners(step):
+        def some(g, offset):
+            core, z = g // 4, g % 4
+            for x in range(4):
+                for y in range(4):
+                    at = {"x": x, "y": y, "z": z}
+                    where = [
+                        core * 64 + at[three] * 16 + at[one] * 4 + at[two]
+                        for one, two, three in AXES
+                    ]
+                    offset = step(where, offset)
+            return offset
+
+        return lax.fori_loop(0, 8, some, jnp.int32(0))
+
+    def pack(where, offset):
         shift = offset % 128
         base = pl.multiple_of(offset - shift, 128)
-        x = jnp.concatenate([unfold((all0[o], all1[o], all2[o])), blank], axis=0)
+        x = unfold([ref[k] for ref, k in zip((all0, all1, all2), where)])
+        x = jnp.concatenate([x, blank], axis=0)
         x = jnp.concatenate([x, jnp.zeros((8, 128), f32)], axis=1)
         x = pltpu.roll(x, shift, 1)
         first = pl.ds(base, 128)
         comp[:, first] = jnp.where(lane < shift, comp[:, first], x[:, 0:128])
         comp[:, pl.ds(base + 128, SLOTS)] = x[:, 128:]
-        return offset + count[0, o]
-
-    total = lax.fori_loop(0, OWNERS, pack, jnp.int32(0), unroll=16)
+        return offset + count[0, where[0]]
+
+    total = owners(pack)
     blocks = (total + BLOCK - 1) // BLOCK
     centre = centre_ref[:, 0:1]
     row = lax.broadcasted_iota(jnp.int32, (8, 1), 0)
@@ -340,16 +347,16 @@
         *[pltpu.ACC(1)((32, BLOCK), f32)] * 2,
     )
 
-    def unpack(o, offset):
+    def unpack(where, offset):
         shift = offset % 128
         base = pl.multiple_of(offset - shift, 128)
         x = sums[:, pl.ds(base, SLOTS + 128)]
         x = pltpu.roll(x, (SLOTS + 128) - shift, 1)
         for p in range(PAIRS):
-            outs[p][o] = fold(x[2 * p:2 * p + 2, 0:SLOTS])
-        return offset + count[0, o]
-
-    lax.fori_loop(0, OWNERS, unpack, jnp.int32(0), unroll=16)
+            outs[p][where[p]] = fold(x[2 * p:2 * p + 2, 0:SLOTS])
+        return offset + count[0, where[0]]
+
+    owners(unpack)
 
 
 def pair_scratch():
@@ -382,59 +389,56 @@
         started.append(c)
         return c
 
-    def plane(p, d):
-        axis = REDUCE_ORDER[p][0][0]
-        return {"x": None, "y": None, "z": None, axis: (me[axis] + d) % 4}
+    def third(p, d):
+        return (me[AXES[p][2]] + d) % 4
 
     pl.semaphore_wait(barrier, 10)
     over = [[None] * PAIRS for _ in range(5)]
     for d in (1, 2, 3, 4):
         for p in range(PAIRS):
             over[d][p] = send(
-                p, 0, d - 1, view(part[p], plane(p, d), 1 - core), got_core[p].at[d - 1],
+                p, 0, d - 1, part[p].at[1 - core, third(p, d)], got_core[p].at[d - 1],
                 device(me, 1 - core),
             )
     first = [[] for _ in range(PAIRS)]
     for d in (1, 2, 3, 4):
         for p in range(PAIRS):
             over[d][p].wait_recv()
-            sum_1[p][d - 1] = view(part[p], plane(p, d), core)[...] + got_core[p][d - 1]
+            sum_1[p][d - 1] = part[p][core, third(p, d)] + got_core[p][d - 1]
             if d < 4:
-                axis = REDUCE_ORDER[p][0][0]
+                axis = AXES[p][2]
                 first[p].append(send(
                     p, 1, d - 1, sum_1[p].at[d - 1], got_1[p].at[d - 1],
                     along(me, core, axis, d),
                 ))
     second = [[] for _ in range(PAIRS)]
     for p in range(PAIRS):
-        axes, _, _, at2, _ = REDUCE_ORDER[p]
+        axis = AXES[p][0]
         for c in first[p]:
             c.wait_recv()
         sum_1[p][3] = sum_1[p][3] + (got_1[p][0] + got_1[p][1] + got_1[p][2])
         for d in (1, 2, 3):
+            line = pl.ds((me[axis] + d) % 4 * 4, 4)
             second[p].append(send(
-                p, 2, d - 1, at2(sum_1[p].at[3], (me[axes[1]] + d) % 4), got_2[p].at[d - 1],
-                along(me, core, axes[1], d),
+                p, 2, d - 1, sum_1[p].at[3, line], got_2[p].at[d - 1], along(me, core, axis, d)
             ))
-    third = [[] for _ in range(PAIRS)]
+    last = [[] for _ in range(PAIRS)]
     for p in range(PAIRS):
-        axes, _, _, at2, at3 = REDUCE_ORDER[p]
+        axis = AXES[p][1]
         for c in second[p]:
             c.wait_recv()
-        own = at2(sum_1[p].at[3], me[axes[1]])[...]
+        own = sum_1[p][3, pl.ds(me[AXES[p][0]] * 4, 4)]
         sum_2[p][...] = own + (got_2[p][0] + got_2[p][1] + got_2[p][2])
         for d in (1, 2, 3):
-            third[p].append(send(
-                p, 3, d - 1, at3(sum_2[p], (me[axes[2]] + d) % 4), got_3[p].at[d - 1],
-                along(me, core, axes[2], d),
+            last[p].append(send(
+                p, 3, d - 1, sum_2[p].at[(me[axis] + d) % 4], got_3[p].at[d - 1],
+                along(me, core, axis, d),
             ))
     blocks = []
     for p in range(PAIRS):
-        axes, _, _, _, at3 = REDUCE_ORDER[p]
-        for c in third[p]:
+        for c in last[p]:
             c.wait_recv()
-        own = at3(sum_2[p], me[axes[2]])[...]
-        blocks.append(own + (got_3[p][0] + got_3[p][1] + got_3[p][2]))
+        blocks.append(sum_2[p][me[AXES[p][1]]] + (got_3[p][0] + got_3[p][1] + got_3[p][2]))
 
     total = unfold(blocks) * (1.0 / (STARS * OWNERS))
     start = start_ref[...]
@@ -456,6 +460,9 @@
     def lines(a):
         return a.reshape(STARS // 128, 128)
 
+    def near(a):
+        return pltpu.with_memory_space_constraint(a, pltpu.VMEM)
+
     def params(collective_id=None):
         extra = {} if collective_id is None else {
             "collective_id": collective_id, "has_side_effects": True
@@ -464,13 +471,13 @@
 
     *every, start, hq, hr, fw, fl, centre = pl.pallas_call(
         gather_kernel,
-        out_shape=[jax.ShapeDtypeStruct(PLACES, f32)] * PAIRS + [
-            jax.ShapeDtypeStruct((16, SLOTS), f32),
-            jax.ShapeDtypeStruct((STARS, 128), bf16),
-            jax.ShapeDtypeStruct((STARS, 128), bf16),
-            jax.ShapeDtypeStruct((16, STARS), bf16),
-            jax.ShapeDtypeStruct((32, STARS), f8),
-            jax.ShapeDtypeStruct((8, 128), f32),
+        out_shape=[pltpu.VMEM(PLACES, f32)] * PAIRS + [
+            pltpu.VMEM((16, SLOTS), f32),
+            pltpu.VMEM((STARS, 128), bf16),
+            pltpu.VMEM((STARS, 128), bf16),
+            pltpu.VMEM((16, STARS), bf16),
+            pltpu.VMEM((32, STARS), f8),
+            pltpu.VMEM((8, 128), f32),
         ],
         in_specs=[vmem()] * 8 + [smem()],
         out_specs=[vmem()] * (PAIRS + 6),
@@ -482,22 +489,25 @@
         compiler_params=params(0),
         name="predict_gather",
     )(
-        positions, velocities, old_acc, old_jerk, lines(masses), lines(elapsed), lines(levels),
-        active_index, active_count,
+        *[
+            pltpu.with_memory_space_constraint(a, pltpu.HBM)
+            for a in (positions, velocities, old_acc, old_jerk, lines(masses), lines(elapsed),
+                      lines(levels), active_index)
+        ],
+        active_count,
     )
     parts = pl.pallas_call(
         pair_kernel,
-        out_shape=[jax.ShapeDtypeStruct((OWNERS, 8, 128), f32)] * PAIRS,
+        out_shape=[pltpu.VMEM((OWNERS, 8, 128), f32)] * PAIRS,
         in_specs=[vmem()] * 8,
         out_specs=[vmem()] * PAIRS,
         scratch_shapes=pair_scratch(),
         compiler_params=params(),
         name="pair_sums",
-    )(*[e.reshape(OWNERS, 8, 128) for e in every], hq, hr, fw, fl, centre)
-
-    def buffers(count, which):
-        head = () if count is None else (count,)
-        return [pltpu.VMEM(head + order[which] + (8, 128), f32) for order in REDUCE_ORDER]
+    )(*[near(e.reshape(OWNERS, 8, 128)) for e in every], near(hq), near(hr), near(fw), near(fl), near(centre))
+
+    def buffers(*shape):
+        return [pltpu.VMEM(shape + (8, 128), f32)] * PAIRS
 
     return pl.pallas_call(
         reduce_kernel,
@@ -505,18 +515,18 @@
         in_specs=[vmem()] * (PAIRS + 1) + [smem()],
         out_specs=vmem(),
         scratch_shapes=[
-            buffers(4, 1),
-            buffers(3, 1),
-            buffers(3, 2),
-            [pltpu.VMEM((3, 8, 128), f32)] * PAIRS,
-            buffers(4, 1),
-            buffers(None, 2),
+            buffers(4, 16),
+            buffers(3, 16),
+            buffers(3, 4),
+            buffers(3),
+            buffers(4, 16),
+            buffers(4),
             pltpu.SemaphoreType.DMA((PAIRS, 4, 4)),
             pltpu.SemaphoreType.DMA((PAIRS, 4, 4)),
         ],
         compiler_params=params(1),
         name="reduce_correct",
-    )(*[p.reshape(PLACES) for p in parts], start, active_count)
+    )(*[near(p.reshape(PLACES)) for p in parts], near(start), active_count)
 
 
 def solution(mesh):

time: 165 us -> 153 us (0.927)
  Pallas kernels: 162 us -> 151 us
    pallas_call x2, Pallas kernels: 145 us -> 136 us  [the longest x1 113 us: shards(): pl.pallas_call(pair_kernel, out_shape=[pltpu.VMEM((OWNERS, 8, 128), f32)]...]
    pallas_call x1, Pallas kernels: 17 us -> 15 us  [shards(): pl.pallas_call(reduce_kernel, out_shape=jax.ShapeDtypeStruct((12, SLOTS),...]
where the time goes in v5:
time: 153 us; the launch traced here: 152 us
  Pallas kernels  151 us (99%)
    pallas_call x1, Pallas kernels, shards(): pl.pallas_call(pair_kernel, out_shape=[pltpu.VMEM((OWNERS, 8, 128), f32)]...  113 us
    pallas_call x1, Pallas kernels, shards(): pl.pallas_call(gather_kernel, out_shape=[pltpu.VMEM(PLACES, f32)] * PAIRS...  22.9 us
    pallas_call x1, Pallas kernels, shards(): pl.pallas_call(reduce_kernel, out_shape=jax.ShapeDtypeStruct((12, SLOTS),...  15 us

profile of v5, /device:TPU:1, one launch (start us, length us, event | category | flops | bytes accessed | tf_op | source)
XLA Modules:
  0.0 151.9 jit_solution(4650323429086212334)
XLA Ops:
  0.7 22.9 %predict_gather.1 = (f32[2,4,16,8,128]{4,3,2,1,0:T(8,128)S(1)}, f32[2,4,16,8,128]{4,3,2,1,0:T(8,128)S(1)}, f32[2,4,16,8,128]{4,3,2,1,0:T(8,128)S(1)}, f32[16,512...) custom-call(f32[3,1536]{1,0:T(4,128)} %pos_ref.1, ...), custom_call_target="tpu_custom_call" | custom-call | tf_op jit(solution)/shard_map/predict_gather/pallas_call | solution.py:472
  23.6 112.7 %pair_sums.1 = (f32[128,8,128]{2,1,0:T(8,128)S(1)}, f32[128,8,128]{2,1,0:T(8,128)S(1)}, f32[128,8,128]{2,1,0:T(8,128)S(1)}) custom-call(f32[128,8,128]{2,1,0:T(8,128)S(1)} %bitcast.9, f32[128,8,128]{2,1,0:T(8,128)S(1)} %bitcast.10, f32[128,8,128]{2,1,0:T(8,128)S(1)} %bitcast.11, bf16[1536,128]{1,0:T(8,128)(2,1)S(1)} %get-tuple-element.20.hq, ...), custom_call_target="tpu_custom_call" | custom-call | tf_op jit(solution)/shard_map/pair_sums/pallas_call | solution.py:499
  136.3 15.0 %reduce_correct.1 = f32[12,512]{1,0:T(8,128)S(1)} custom-call(f32[2,4,16,8,128]{4,3,2,1,0:T(8,128)S(1)} %bitcast.12, f32[2,4,16,8,128]{4,3,2,1,0:T(8,128)S(1)} %bitcast.13, f32[2,4,16,8,128]{4,3,2,1,0:T(8,128)S(1)} %bitcast.14, f32[16,512]{1,0:T(8,128)S(1)} %get-tuple-element.28.start_ref, s32[1]{0:T(128)S(6)} %copy.11.count_ref), custom_call_target="tpu_custom_call" | custom-call | tf_op jit(solution)/shard_map/reduce_correct/pallas_call | solution.py:512
  151.3 0.6 copy.12

commit v6 on v5

--- a/solution.py
+++ b/solution.py
@@ -13,14 +13,17 @@
 
 STARS = 1536
 SLOTS = 512
+SOURCES = 2 * STARS
+HALF = SLOTS // 2
 OWNERS = 128
 BLOCK = 256
 CHUNK = 256
-ROOM = OWNERS * SLOTS + SLOTS + 128
+TURN = 2
+ROOM = OWNERS * HALF + HALF + 128
 VMEM_LIMIT = 24 * 2**20
 PAIRS = 3
 AXES = ("xyz", "yzx", "zxy")
-PLACES = (2, 4, 16, 8, 128)
+PLACES = (4, 16, 2, 4, 128)
 POS_SCALE = 2.0**-2
 VEL_SCALE = 2.0**-8
 W_SCALE = 2.0**6
@@ -57,10 +60,10 @@
 def greet():
     me, core = place()
     barrier = pltpu.get_barrier_semaphore()
-    peers = [along(me, core, axis, d) for axis in "xyz" for d in (1, 2, 3)]
+    peers = [along(me, c, axis, d) for c in (core, 1 - core) for axis in "xyz" for d in (1, 2, 3)]
     for peer in [device(me, 1 - core)] + peers:
         pl.semaphore_signal(barrier, inc=1, device_id=peer, device_id_type=MESH)
-    return barrier
+    return barrier, 1 + len(peers)
 
 
 def predict(d, step):
@@ -76,29 +79,43 @@
 
 
 def fold(rows):
-    return jnp.concatenate([rows[:, 128 * t:128 * (t + 1)] for t in range(4)], axis=0)
+    return jnp.concatenate([rows[:, 128 * t:128 * (t + 1)] for t in range(2)], axis=0)
 
 
 def unfold(blocks):
     return jnp.concatenate(
-        [jnp.concatenate([b[2 * t:2 * t + 2] for b in blocks], axis=0) for t in range(4)], axis=1
+        [jnp.concatenate([b[2 * t:2 * t + 2] for b in blocks], axis=0) for t in range(2)], axis=1
     )
+
+
+def slot_of(shape, axis):
+    j = lax.broadcasted_iota(jnp.int32, shape, axis)
+    return jnp.where(j < HALF, 2 * j, 2 * j - (SLOTS - 1))
+
+
+def reorder(rows, back):
+    own = lax.broadcasted_iota(jnp.int32, (SLOTS, SLOTS), 1 if back else 0)
+    move = (own == slot_of((SLOTS, SLOTS), 0 if back else 1)).astype(f32).astype(bf16)
+    n = rows.shape[0]
+    parts = jnp.concatenate(split3(rows), axis=0).astype(bf16)
+    out = jnp.dot(parts, move, preferred_element_type=f32)
+    return (out[0:n] + out[n:2 * n]) + out[2 * n:3 * n]
 
 
 def gather_kernel(
     pos_ref, vel_ref, acc_ref, jerk_ref, mass_ref, elapsed_ref, levels_ref, index_ref, count_ref,
     all0, all1, all2, start_ref, hq_ref, hr_ref, fw_ref, f8_ref, centre_ref,
-    state, send_sem, recv_sem,
+    state, src_ref, other, send_sem, recv_sem,
 ):
     every = (all0, all1, all2)
-    barrier = greet()
+    barrier, greeted = greet()
     me, core = place()
     started = []
 
-    def send(p, phase, k, block, target):
+    def send(p, k, src, dst, target):
         c = pltpu.make_async_remote_copy(
-            src_ref=block, dst_ref=block, send_sem=send_sem.at[p, phase, k],
-            recv_sem=recv_sem.at[p, phase, k], device_id=target, device_id_type=MESH,
+            src_ref=src, dst_ref=dst, send_sem=send_sem.at[p, k],
+            recv_sem=recv_sem.at[p, k], device_id=target, device_id_type=MESH,
         )
         c.start()
         started.append(c)
@@ -123,27 +140,37 @@
     start_ref[...] = start
     target = jnp.concatenate(predict(start, start[12:13]), axis=0)
     live = lax.broadcasted_iota(jnp.int32, (8, SLOTS), 1) < count_ref[0]
-    pairs = (jnp.where(live[0:2], target[0:2], 1e30), target[2:4], target[4:6])
+    target = reorder(jnp.concatenate([target, jnp.zeros((2, SLOTS), f32)], axis=0), False)
+    marks = slot_of((8, SLOTS), 1) < count_ref[0]
+    pairs = (jnp.where(marks[0:2], target[0:2], 1e30), target[2:4], target[4:6])
     for p in range(PAIRS):
         one, two, three = (me[axis] for axis in AXES[p])
-        every[p][core, three, one * 4 + two] = fold(pairs[p])
-
-    pl.semaphore_wait(barrier, 10)
+        even, odd = fold(pairs[p][:, 0:HALF]), fold(pairs[p][:, HALF:])
+        every[p][three, one * 4 + two, core] = jnp.where(core == 0, even, odd)
+        other[p] = jnp.where(core == 0, odd, even)
+
+    pl.semaphore_wait(barrier, greeted)
 
     flight = [[] for _ in range(PAIRS)]
 
     def begin(phase):
         for p in range(PAIRS):
             one, two, three = (me[axis] for axis in AXES[p])
-            block = every[p].at[core, three]
+            block = every[p].at[three]
             if phase == 0:
-                block = block.at[one * 4 + two]
+                block = block.at[one * 4 + two, core]
             elif phase == 1:
                 block = block.at[pl.ds(one * 4, 4)]
             axis = AXES[p][(1, 0, 2)[phase]]
             flight[p] = [
-                send(p, phase, d - 1, block, along(me, core, axis, d)) for d in (1, 2, 3)
+                send(p, 3 * phase + d - 1, block, block, along(me, core, axis, d))
+                for d in (1, 2, 3)
             ]
+            if phase == 0:
+                flight[p] += [
+                    send(p, 9 + d, other.at[p], block, along(me, 1 - core, axis, d))
+                    for d in range(4)
+                ]
 
     def finish():
         for p in range(PAIRS):
@@ -157,16 +184,23 @@
     )[0:1]
     interval = jnp.where(chosen > 0.5, step, flat(elapsed_ref))
     src = jnp.concatenate(predict(state[...], interval), axis=0)
+    mass = flat(mass_ref)
+    src_ref[core] = jnp.concatenate([src, mass, jnp.zeros_like(mass)], axis=0)
+    share = send(0, 13, src_ref.at[core], src_ref.at[core], device(me, 1 - core))
     finish()
     begin(1)
-
-    centre = jnp.sum(src, axis=1, keepdims=True) * (1.0 / STARS)
+    share.wait_recv()
+
+    src = jnp.concatenate([src_ref[0], src_ref[1]], axis=1)
+    mass = src[6:7]
+    src = src[0:6]
+    centre = jnp.sum(src, axis=1, keepdims=True) * (1.0 / SOURCES)
     centre = jnp.floor(centre * 64.0 + 0.5) * (1.0 / 64.0)
     src = src - centre
     centre = jnp.concatenate([centre, jnp.zeros((2, 1), f32)], axis=0)
     centre_ref[...] = jnp.broadcast_to(centre, (8, 128))
-    zero = jnp.zeros((1, STARS), f32)
-    weights = jnp.concatenate([src, zero + 1.0, zero], axis=0) * flat(mass_ref)
+    zero = jnp.zeros((1, SOURCES), f32)
+    weights = jnp.concatenate([src, zero + 1.0, zero], axis=0) * mass
     pos, vel = src[0:3] * POS_SCALE, src[3:6] * VEL_SCALE
     row = lax.broadcasted_iota(jnp.int32, (8, 1), 0)
 
@@ -174,32 +208,21 @@
         a, b, c = split3(jnp.concatenate([own, zero, zero], axis=0))
         a = a + (row == unit).astype(f32)
         s = jnp.concatenate(split3(square) + (zero,) * 5, axis=0)
-        fill = jnp.zeros((72, STARS), f32)
+        fill = jnp.zeros((72, SOURCES), f32)
         return jnp.concatenate([a, b, a, b, c, a, s, fill], axis=0).T.astype(bf16)
 
     square = pos[0:1] * pos[0:1] + pos[1:2] * pos[1:2] + pos[2:3] * pos[2:3]
     hq_ref[...] = factors(jnp.concatenate([pos * -2.0, zero, zero, zero], axis=0), square, 6)
     finish()
     begin(2)
-    over = [
-        [send(p, 3, 0, every[p].at[core, me[AXES[p][2]]], device(me, 1 - core))]
-        for p in range(PAIRS)
-    ]
     product = pos[0:1] * vel[0:1] + pos[1:2] * vel[1:2] + pos[2:3] * vel[2:3]
     hr_ref[...] = factors(jnp.concatenate([-vel, -pos], axis=0), product, 7)
-    fill = jnp.zeros((8, STARS), f32)
+    fill = jnp.zeros((8, SOURCES), f32)
     fw_ref[...] = jnp.concatenate(split3(weights)[0:2], axis=0).astype(bf16)
     high = weights.astype(f8).astype(f32)
     f8_ref[...] = jnp.concatenate([high, weights - high, fill, fill], axis=0).astype(f8)
 
-    for d in (1, 2, 3):
-        for p in range(PAIRS):
-            flight[p][d - 1].wait_recv()
-            came = (me[AXES[p][2]] - d + 4) % 4
-            over[p].append(send(p, 3, d, every[p].at[core, came], device(me, 1 - core)))
-    for p in range(PAIRS):
-        for c in over[p]:
-            c.wait_recv()
+    finish()
     for c in started:
         c.wait_send()
 
@@ -219,16 +242,16 @@
     copy.wait()
 
     lane = lax.broadcasted_iota(jnp.int32, (8, 128), 1)
-    blank = jnp.zeros((2, SLOTS), f32)
+    blank = jnp.zeros((2, HALF), f32)
 
     def owners(step):
         def some(g, offset):
-            core, z = g // 4, g % 4
+            core, z = g % 2, g // 2
             for x in range(4):
                 for y in range(4):
                     at = {"x": x, "y": y, "z": z}
                     where = [
-                        core * 64 + at[three] * 16 + at[one] * 4 + at[two]
+                        (at[three] * 16 + at[one] * 4 + at[two]) * 2 + core
                         for one, two, three in AXES
                     ]
                     offset = step(where, offset)
@@ -245,7 +268,7 @@
         x = pltpu.roll(x, shift, 1)
         first = pl.ds(base, 128)
         comp[:, first] = jnp.where(lane < shift, comp[:, first], x[:, 0:128])
-        comp[:, pl.ds(base + 128, SLOTS)] = x[:, 128:]
+        comp[:, pl.ds(base + 128, HALF)] = x[:, 128:]
         return offset + count[0, where[0]]
 
     total = owners(pack)
@@ -293,9 +316,9 @@
             raw[32:64] = pltpu.matmul_pop(acc_lw)
             raw[64:96] = pltpu.matmul_pop(acc_lb)
 
-        chunks = STARS // CHUNK
-
-        def block(i, carry):
+        chunks = SOURCES // CHUNK
+
+        def block(i):
             for c in range(chunks):
                 if c == chunks - 1:
                     stage_factor(i + 1)
@@ -325,6 +348,10 @@
                 pltpu.matmul_acc_lhs(acc_lb, fl[:, part], load_staged_rhs=1)
                 if c == 0:
                     combine(jnp.maximum(i - 1, 0))
+
+        def several(j, carry):
+            for k in range(TURN):
+                block(j * TURN + k)
             return carry
 
         pop_sums()
@@ -333,7 +360,13 @@
             pltpu.matmul_pop(acc_r[k])
         stage_factor(0)
         stage_one(0, 0, 0)
-        lax.fori_loop(0, blocks, block, 0)
+        lax.fori_loop(0, blocks // TURN, several, 0)
+
+        def single(i, carry):
+            block(i)
+            return carry
+
+        lax.fori_loop(blocks // TURN * TURN, blocks, single, 0)
         pltpu.matmul_pop(acc_q[0])
         pltpu.matmul_pop(acc_r[0])
         pop_sums()
@@ -350,10 +383,10 @@
     def unpack(where, offset):
         shift = offset % 128
         base = pl.multiple_of(offset - shift, 128)
-        x = sums[:, pl.ds(base, SLOTS + 128)]
-        x = pltpu.roll(x, (SLOTS + 128) - shift, 1)
+        x = sums[:, pl.ds(base, HALF + 128)]
+        x = pltpu.roll(x, (HALF + 128) - shift, 1)
         for p in range(PAIRS):
-            outs[p][where[p]] = fold(x[2 * p:2 * p + 2, 0:SLOTS])
+            outs[p][where[p]] = fold(x[2 * p:2 * p + 2, 0:HALF])
         return offset + count[0, where[0]]
 
     owners(unpack)
@@ -373,74 +406,76 @@
 
 def reduce_kernel(
     part0, part1, part2, start_ref, count_ref, out_ref,
-    got_core, got_1, got_2, got_3, sum_1, sum_2, send_sem, recv_sem,
+    got_1, got_2, got_3, got_other, sum_1, sum_2, send_sem, recv_sem,
 ):
     part = (part0, part1, part2)
-    barrier = greet()
+    barrier, greeted = greet()
     me, core = place()
     started = []
 
-    def send(p, phase, k, src, dst, target):
+    def send(p, k, src, dst, target):
         c = pltpu.make_async_remote_copy(
-            src_ref=src, dst_ref=dst, send_sem=send_sem.at[p, phase, k],
-            recv_sem=recv_sem.at[p, phase, k], device_id=target, device_id_type=MESH,
+            src_ref=src, dst_ref=dst, send_sem=send_sem.at[p, k],
+            recv_sem=recv_sem.at[p, k], device_id=target, device_id_type=MESH,
         )
         c.start()
         started.append(c)
         return c
 
-    def third(p, d):
-        return (me[AXES[p][2]] + d) % 4
-
-    pl.semaphore_wait(barrier, 10)
-    over = [[None] * PAIRS for _ in range(5)]
-    for d in (1, 2, 3, 4):
-        for p in range(PAIRS):
-            over[d][p] = send(
-                p, 0, d - 1, part[p].at[1 - core, third(p, d)], got_core[p].at[d - 1],
-                device(me, 1 - core),
-            )
+    pl.semaphore_wait(barrier, greeted)
     first = [[] for _ in range(PAIRS)]
-    for d in (1, 2, 3, 4):
-        for p in range(PAIRS):
-            over[d][p].wait_recv()
-            sum_1[p][d - 1] = part[p][core, third(p, d)] + got_core[p][d - 1]
-            if d < 4:
-                axis = AXES[p][2]
-                first[p].append(send(
-                    p, 1, d - 1, sum_1[p].at[d - 1], got_1[p].at[d - 1],
-                    along(me, core, axis, d),
-                ))
+    for p in range(PAIRS):
+        axis = AXES[p][2]
+        for d in (1, 2, 3):
+            first[p].append(send(
+                p, d - 1, part[p].at[(me[axis] + d) % 4], got_1[p].at[d - 1],
+                along(me, core, axis, d),
+            ))
     second = [[] for _ in range(PAIRS)]
     for p in range(PAIRS):
         axis = AXES[p][0]
         for c in first[p]:
             c.wait_recv()
-        sum_1[p][3] = sum_1[p][3] + (got_1[p][0] + got_1[p][1] + got_1[p][2])
+        own = part[p][me[AXES[p][2]]]
+        sum_1[p][...] = own + (got_1[p][0] + got_1[p][1] + got_1[p][2])
         for d in (1, 2, 3):
             line = pl.ds((me[axis] + d) % 4 * 4, 4)
             second[p].append(send(
-                p, 2, d - 1, sum_1[p].at[3, line], got_2[p].at[d - 1], along(me, core, axis, d)
+                p, 2 + d, sum_1[p].at[line], got_2[p].at[d - 1], along(me, core, axis, d)
             ))
     last = [[] for _ in range(PAIRS)]
     for p in range(PAIRS):
         axis = AXES[p][1]
         for c in second[p]:
             c.wait_recv()
-        own = sum_1[p][3, pl.ds(me[AXES[p][0]] * 4, 4)]
+        own = sum_1[p][pl.ds(me[AXES[p][0]] * 4, 4)]
         sum_2[p][...] = own + (got_2[p][0] + got_2[p][1] + got_2[p][2])
         for d in (1, 2, 3):
             last[p].append(send(
-                p, 3, d - 1, sum_2[p].at[(me[axis] + d) % 4], got_3[p].at[d - 1],
+                p, 5 + d, sum_2[p].at[(me[axis] + d) % 4, core], got_3[p].at[d - 1],
                 along(me, core, axis, d),
             ))
-    blocks = []
+        for d in range(4):
+            last[p].append(send(
+                p, 9 + d, sum_2[p].at[(me[axis] + d) % 4, 1 - core], got_other[p].at[d],
+                along(me, 1 - core, axis, d),
+            ))
+    mine, others = [], []
     for p in range(PAIRS):
         for c in last[p]:
             c.wait_recv()
-        blocks.append(sum_2[p][me[AXES[p][1]]] + (got_3[p][0] + got_3[p][1] + got_3[p][2]))
-
-    total = unfold(blocks) * (1.0 / (STARS * OWNERS))
+        own = sum_2[p][me[AXES[p][1]], core]
+        mine.append(own + (got_3[p][0] + got_3[p][1] + got_3[p][2]))
+        others.append(
+            (got_other[p][0] + got_other[p][1]) + (got_other[p][2] + got_other[p][3])
+        )
+    mine, others = unfold(mine), unfold(others)
+    halves = [jnp.where(core == 0, mine, others), jnp.where(core == 0, others, mine)]
+    total = jnp.concatenate(
+        [jnp.concatenate(halves, axis=1), jnp.zeros((2, SLOTS), f32)], axis=0
+    )
+    total = jnp.where(slot_of((8, SLOTS), 1) < count_ref[0], total, 0.0)
+    total = reorder(total, True) * (1.0 / (STARS * OWNERS))
     start = start_ref[...]
     step = start[12:13]
     acc0, jerk0 = start[6:9], start[9:12]
@@ -473,18 +508,20 @@
         gather_kernel,
         out_shape=[pltpu.VMEM(PLACES, f32)] * PAIRS + [
             pltpu.VMEM((16, SLOTS), f32),
-            pltpu.VMEM((STARS, 128), bf16),
-            pltpu.VMEM((STARS, 128), bf16),
-            pltpu.VMEM((16, STARS), bf16),
-            pltpu.VMEM((32, STARS), f8),
+            pltpu.VMEM((SOURCES, 128), bf16),
+            pltpu.VMEM((SOURCES, 128), bf16),
+            pltpu.VMEM((16, SOURCES), bf16),
+            pltpu.VMEM((32, SOURCES), f8),
             pltpu.VMEM((8, 128), f32),
         ],
         in_specs=[vmem()] * 8 + [smem()],
         out_specs=[vmem()] * (PAIRS + 6),
         scratch_shapes=[
             pltpu.VMEM((16, STARS), f32),
-            pltpu.SemaphoreType.DMA((PAIRS, 4, 4)),
-            pltpu.SemaphoreType.DMA((PAIRS, 4, 4)),
+            pltpu.VMEM((2, 8, STARS), f32),
+            pltpu.VMEM((PAIRS, 4, 128), f32),
+            pltpu.SemaphoreType.DMA((PAIRS, 14)),
+            pltpu.SemaphoreType.DMA((PAIRS, 14)),
         ],
         compiler_params=params(0),
         name="predict_gather",
@@ -498,16 +535,16 @@
     )
     parts = pl.pallas_call(
         pair_kernel,
-        out_shape=[pltpu.VMEM((OWNERS, 8, 128), f32)] * PAIRS,
+        out_shape=[pltpu.VMEM((OWNERS, 4, 128), f32)] * PAIRS,
         in_specs=[vmem()] * 8,
         out_specs=[vmem()] * PAIRS,
         scratch_shapes=pair_scratch(),
         compiler_params=params(),
         name="pair_sums",
-    )(*[near(e.reshape(OWNERS, 8, 128)) for e in every], near(hq), near(hr), near(fw), near(fl), near(centre))
+    )(*[near(e.reshape(OWNERS, 4, 128)) for e in every], near(hq), near(hr), near(fw), near(fl), near(centre))
 
     def buffers(*shape):
-        return [pltpu.VMEM(shape + (8, 128), f32)] * PAIRS
+        return [pltpu.VMEM(shape + (4, 128), f32)] * PAIRS
 
     return pl.pallas_call(
         reduce_kernel,
@@ -515,14 +552,14 @@
         in_specs=[vmem()] * (PAIRS + 1) + [smem()],
         out_specs=vmem(),
         scratch_shapes=[
-            buffers(4, 16),
-            buffers(3, 16),
-            buffers(3, 4),
+            buffers(3, 16, 2),
+            buffers(3, 4, 2),
             buffers(3),
-            buffers(4, 16),
             buffers(4),
-            pltpu.SemaphoreType.DMA((PAIRS, 4, 4)),
-            pltpu.SemaphoreType.DMA((PAIRS, 4, 4)),
+            buffers(16, 2),
+            buffers(4, 2),
+            pltpu.SemaphoreType.DMA((PAIRS, 14)),
+            pltpu.SemaphoreType.DMA((PAIRS, 14)),
         ],
         compiler_params=params(1),
         name="reduce_correct",

time: 153 us -> 155 us (1.013)
  Pallas kernels: 151 us -> 154 us
    pallas_call x1, Pallas kernels: 113 us -> 117 us  [shards(): pl.pallas_call(pair_kernel, out_shape=[pltpu.VMEM((OWNERS, 4, 128), f32)]...]
    pallas_call x1, Pallas kernels: 22.9 us -> 19.9 us  [shards(): pl.pallas_call(gather_kernel, out_shape=[pltpu.VMEM(PLACES, f32)] * PAIRS...]
    pallas_call x1, Pallas kernels: 15 us -> 17.3 us  [shards(): pl.pallas_call(reduce_kernel, out_shape=jax.ShapeDtypeStruct((12, SLOTS),...]
where the time goes in v6:
time: 155 us
  Pallas kernels  154 us (99%)
    pallas_call x1, Pallas kernels, shards(): pl.pallas_call(pair_kernel, out_shape=[pltpu.VMEM((OWNERS, 4, 128), f32)]...  117 us
    pallas_call x1, Pallas kernels, shards(): pl.pallas_call(gather_kernel, out_shape=[pltpu.VMEM(PLACES, f32)] * PAIRS...  19.9 us
    pallas_call x1, Pallas kernels, shards(): pl.pallas_call(reduce_kernel, out_shape=jax.ShapeDtypeStruct((12, SLOTS),...  17.3 us

profile of v6, /device:TPU:1, one launch (start us, length us, event | category | flops | bytes accessed | tf_op | source)
XLA Modules:
  0.0 155.3 jit_solution(5184059722315910719)
XLA Ops:
  0.7 19.9 %predict_gather.1 = (f32[4,16,2,4,128]{4,3,2,1,0:T(4,128)S(1)}, f32[4,16,2,4,128]{4,3,2,1,0:T(4,128)S(1)}, f32[4,16,2,4,128]{4,3,2,1,0:T(4,128)S(1)}, f32[16,512...) custom-call(f32[3,1536]{1,0:T(4,128)} %pos_ref.1, ...), custom_call_target="tpu_custom_call" | custom-call | tf_op jit(solution)/shard_map/predict_gather/pallas_call | solution.py:507
  20.5 116.8 %pair_sums.1 = (f32[128,4,128]{2,1,0:T(4,128)S(1)}, f32[128,4,128]{2,1,0:T(4,128)S(1)}, f32[128,4,128]{2,1,0:T(4,128)S(1)}) custom-call(f32[128,4,128]{2,1,0:T(4,128)S(1)} %bitcast.12, f32[128,4,128]{2,1,0:T(4,128)S(1)} %bitcast.13, f32[128,4,128]{2,1,0:T(4,128)S(1)} %bitcast.14, bf16[3072,128]{1,0:T(8,128)(2,1)S(1)} %get-tuple-element.20.hq, ...), custom_call_target="tpu_custom_call" | custom-call | tf_op jit(solution)/shard_map/pair_sums/pallas_call | solution.py:536
  137.3 17.3 %reduce_correct.1 = f32[12,512]{1,0:T(8,128)S(1)} custom-call(f32[4,16,2,4,128]{4,3,2,1,0:T(4,128)S(1)} %bitcast.9, f32[4,16,2,4,128]{4,3,2,1,0:T(4,128)S(1)} %bitcast.10, f32[4,16,2,4,128]{4,3,2,1,0:T(4,128)S(1)} %bitcast.11, f32[16,512]{1,0:T(8,128)S(1)} %get-tuple-element.28.start_ref, s32[1]{0:T(128)S(6)} %copy.11.count_ref), custom_call_target="tpu_custom_call" | custom-call | tf_op jit(solution)/shard_map/reduce_correct/pallas_call | solution.py:549
  154.7 0.6 copy.12
